TPU v7x, 32 devices: a whole 2x2x4 slice. The times are simulated.
32 devices in a mesh: dp: 8 (over y, x, core), replica: 4 (over z).
Axes of the slice: x: 2, y: 2, z: 4, core: 2. Of those that a mesh axis runs over, the one named last changes fastest.
Arguments:
- tokens: bfloat16 [128, 128, 768], P(('dp', 'replica')), may hold values from -6 to 6
- encodings: bfloat16 [128, 64, 768], P(('dp', 'replica')), may hold values from -6 to 6
- lengths: int32 [128], P(('dp', 'replica')), may hold values from 1 to 128, 8192 in all
- memory_ids: int32 [128, 10], P(('dp', 'replica')), may hold values from 0 to 31, all different within a row
- memory_keys: bfloat16 [32, 768], replicated, may hold values from -6 to 6
- memory_values: bfloat16 [32, 768], replicated, may hold values from -6 to 6
- gain_self: float32 [768], replicated, may hold values from 0.5 to 1.5
- gain_cross: float32 [768], replicated, may hold values from 0.5 to 1.5
- gain_ff: float32 [768], replicated, may hold values from 0.5 to 1.5
- rel_bias: float32 [32, 12], replicated, may hold values from -4 to 4
- self_qkv: bfloat16 [768, 2304], replicated, may hold values from -0.109375 to 0.109375
- self_out: bfloat16 [768, 768], replicated, may hold values from -0.875 to 0.875
- cross_q: bfloat16 [768, 768], replicated, may hold values from -0.0546875 to 0.0546875
- cross_kv: bfloat16 [768, 1536], replicated, may hold values from -0.21875 to 0.21875
- cross_out: bfloat16 [768, 768], replicated, may hold values from -0.875 to 0.875
- ff_in: bfloat16 [768, 3072], replicated, may hold values from -0.21875 to 0.21875
- ff_out: bfloat16 [3072, 768], replicated, may hold values from -0.109375 to 0.109375
- cotangent: bfloat16 [128, 128, 768], P(('dp', 'replica')), may hold values from -6 to 6
Outputs:
- layer_output: bfloat16 [128, 128, 768], P(('dp', 'replica'))
- grad_tokens: bfloat16 [128, 128, 768], P(('dp', 'replica'))
- grad_encodings: bfloat16 [128, 64, 768], P(('dp', 'replica'))
- grad_gain_self: float32 [768], P('dp')
- grad_gain_cross: float32 [768], P('dp')
- grad_gain_ff: float32 [768], P('dp')
- grad_rel_bias: float32 [32, 12], replicated
- grad_self_qkv: float32 [768, 2304], P('dp')
- grad_self_out: float32 [768, 768], P('dp')
- grad_cross_q: float32 [768, 768], P('dp')
- grad_cross_kv: float32 [768, 1536], P('dp')
- grad_cross_out: float32 [768, 768], P('dp')
- grad_ff_in: float32 [768, 3072], P('dp')
- grad_ff_out: float32 [3072, 768], P('dp')
- grad_memory_keys: float32 [32, 768], P('dp')
- grad_memory_values: float32 [32, 768], P('dp')
Inputs may be any that keep to these rules, and one draw needn't show every extreme that they name: `lengths`: some question fills all 128 slots. `memory_ids`: each question names 10 different memory entries.
All inputs are finite; a program needn't handle non-finite values. No bound on the sum of `lengths` on one device may be relied on, other than what follows from the above.
Results may differ from a plain program's by a relative error of at most 0.023.
The roundings to bfloat16 on the way count: a program that leaves them out, or rounds other values in their place, can miss the bound.
Values sent between devices are 32-bit elements; how exact they have to be, the bound alone decides.
A program may use at most 192 MiB of HBM per device.

v0:
```python
import jax
import jax.numpy as jnp
import numpy as np
from jax import lax
from jax.sharding import PartitionSpec as P

MAXDIST = 128


EPSILON = 1e-06
NEGATIVE = -1000000000.0


def bucket_table(length, buckets, distance):
    exact = buckets // 2
    apart = np.arange(length)[:, None] - np.arange(length)[None, :]
    apart = np.maximum(apart, 0)
    spread = np.log(np.maximum(apart, 1) / exact) / np.log(distance / exact) * (buckets - exact)
    larger = np.minimum(exact + np.floor(np.maximum(spread, 0.0)).astype(np.int64), buckets - 1)
    return np.where(apart < exact, apart, larger).astype(np.int32)


def rms_norm(values, gain):
    return values * lax.rsqrt(jnp.mean(values * values, axis=-1, keepdims=True) + EPSILON) * gain


def norm_back(values, gain, upstream):
    unused_out, pull = jax.vjp(rms_norm, values, gain)
    d_values, d_gain = pull(upstream)
    return (d_values, d_gain)


def gelu_exact(values):
    return jax.nn.gelu(values, approximate=False)


def gelu_back(values, upstream):
    unused_out, pull = jax.vjp(gelu_exact, values)
    return pull(upstream)[0]


def matmul_plain(left, right):
    return jnp.dot(left, right, preferred_element_type=jnp.float32)


def contract_rows(left, right):
    return lax.dot_general(
        left, right, (((0,), (0,)), ((), ())), preferred_element_type=jnp.float32
    )


def matmul_right_t(left, right):
    return lax.dot_general(
        left, right, (((1,), (1,)), ((), ())), preferred_element_type=jnp.float32
    )


def own_rows(vector):
    rows = vector.shape[0] // lax.axis_size("dp")
    return lax.dynamic_slice_in_dim(vector, lax.axis_index("dp") * rows, rows, 0)


def on_device(
    tokens,
    encodings,
    lengths,
    memory_ids,
    memory_keys,
    memory_values,
    gain_self,
    gain_cross,
    gain_ff,
    rel_bias,
    self_qkv,
    self_out,
    cross_q,
    cross_kv,
    cross_out,
    ff_in,
    ff_out,
    cotangent,
):
    questions, length, width = tokens.shape
    enc_len = encodings.shape[1]
    top_count = memory_ids.shape[1]
    num_buckets, heads = rel_bias.shape
    head_dim = width // heads
    token_rows = questions * length
    mem_rows = memory_keys.shape[0]
    positions = jnp.arange(length)
    causal = positions[None, :] <= positions[:, None]
    valid = (positions[None, :] < lengths[:, None]).reshape(token_rows, 1)
    buckets = jnp.asarray(bucket_table(length, num_buckets, MAXDIST)).astype(jnp.int32)
    one_hot = (buckets[:, :, None] == jnp.arange(num_buckets)[None, None, :]).astype(jnp.float32)
    pos_bias = jnp.transpose(rel_bias[buckets], (2, 0, 1))
    tok_flat = tokens.reshape(token_rows, width).astype(jnp.float32)
    normed_one = rms_norm(tok_flat, gain_self).astype(jnp.bfloat16)
    qkv_all = (
        matmul_plain(normed_one, self_qkv)
        .astype(jnp.bfloat16)
        .reshape(questions, length, 3, heads, head_dim)
    )
    queries, key_rows, val_rows = (qkv_all[:, :, 0], qkv_all[:, :, 1], qkv_all[:, :, 2])

    def self_scores():
        raw = (
            jnp.einsum("qthe,quhe->qhtu", queries, key_rows, preferred_element_type=jnp.float32)
            + pos_bias[None]
        )
        return jnp.where(causal[None, None], raw, NEGATIVE)

    scores = self_scores()
    self_lse = jax.nn.logsumexp(scores, axis=-1, keepdims=True)
    probs = jnp.exp(scores - self_lse)
    attended = jnp.einsum(
        "qhtu,quhe->qthe", probs.astype(jnp.bfloat16), val_rows, preferred_element_type=jnp.float32
    )
    attended = attended.astype(jnp.bfloat16).reshape(token_rows, width)
    hidden_one = tok_flat + matmul_plain(attended, self_out)
    normed_two = rms_norm(hidden_one, gain_cross).astype(jnp.bfloat16)
    cross_query = (
        matmul_plain(normed_two, cross_q)
        .astype(jnp.bfloat16)
        .reshape(questions, length, heads, head_dim)
    )
    enc_flat = encodings.reshape(questions * enc_len, width)
    enc_kv = (
        matmul_plain(enc_flat, cross_kv).astype(jnp.bfloat16).reshape(questions, enc_len, 2 * width)
    )
    mem_keys = jnp.take(memory_keys, memory_ids, axis=0)
    mem_vals = jnp.take(memory_values, memory_ids, axis=0)
    key_count = top_count + enc_len
    all_keys = jnp.concatenate([mem_keys, enc_kv[:, :, :width]], axis=1).reshape(
        questions, key_count, heads, head_dim
    )
    all_vals = jnp.concatenate([mem_vals, enc_kv[:, :, width:]], axis=1).reshape(
        questions, key_count, heads, head_dim
    )

    def cross_scores_of():
        return jnp.einsum(
            "qthe,qkhe->qhtk", cross_query, all_keys, preferred_element_type=jnp.float32
        )

    cross_scores = cross_scores_of()
    cross_lse = jax.nn.logsumexp(cross_scores, axis=-1, keepdims=True)
    cross_probs = jnp.exp(cross_scores - cross_lse)
    cross_att = jnp.einsum(
        "qhtk,qkhe->qthe",
        cross_probs.astype(jnp.bfloat16),
        all_vals,
        preferred_element_type=jnp.float32,
    )
    cross_att = cross_att.astype(jnp.bfloat16).reshape(token_rows, width)
    hidden_two = hidden_one + matmul_plain(cross_att, cross_out)
    normed_three = rms_norm(hidden_two, gain_ff).astype(jnp.bfloat16)
    pre_act = matmul_plain(normed_three, ff_in)
    inner = gelu_exact(pre_act).astype(jnp.bfloat16)
    final = hidden_two + matmul_plain(inner, ff_out)
    layer_output = (
        jnp.where(valid, final, 0.0).astype(jnp.bfloat16).reshape(questions, length, width)
    )
    grad_rows = jnp.where(valid, cotangent.reshape(token_rows, width).astype(jnp.float32), 0.0)
    grad_low = grad_rows.astype(jnp.bfloat16)
    d_ff_out = contract_rows(inner, grad_low)
    d_inner = matmul_right_t(grad_low, ff_out).astype(jnp.bfloat16)
    d_pre = gelu_back(pre_act, d_inner.astype(jnp.float32)).astype(jnp.bfloat16)
    d_ff_in = contract_rows(normed_three, d_pre)
    d_normed_three = matmul_right_t(d_pre, ff_in)
    d_back_three, d_gain_ff = norm_back(hidden_two, gain_ff, d_normed_three)
    grad_two = grad_rows + d_back_three
    ff_a, ff_b = (
        lax.psum_scatter(d_ff_in, "dp", scatter_dimension=0, tiled=True),
        lax.psum_scatter(d_ff_out, "dp", scatter_dimension=0, tiled=True),
    )
    sum_ff_in, sum_ff_out = lax.psum((ff_a, ff_b), "replica")
    branch_two = grad_two.astype(jnp.bfloat16)
    d_cross_out = contract_rows(cross_att, branch_two)
    d_cross_att = (
        matmul_right_t(branch_two, cross_out)
        .astype(jnp.bfloat16)
        .reshape(questions, length, heads, head_dim)
    )
    cross_again = jnp.exp(cross_scores_of() - cross_lse)
    d_all_vals = jnp.einsum(
        "qhtk,qthe->qkhe",
        cross_again.astype(jnp.bfloat16),
        d_cross_att,
        preferred_element_type=jnp.float32,
    )
    d_cross_probs = jnp.einsum(
        "qthe,qkhe->qhtk", d_cross_att, all_vals, preferred_element_type=jnp.float32
    )
    cross_delta = jnp.sum(cross_again * d_cross_probs, axis=-1, keepdims=True)
    d_cross_scores = (cross_again * (d_cross_probs - cross_delta)).astype(jnp.bfloat16)
    d_query = jnp.einsum(
        "qhtk,qkhe->qthe", d_cross_scores, all_keys, preferred_element_type=jnp.float32
    )
    d_query = d_query.astype(jnp.bfloat16).reshape(token_rows, width)
    d_all_keys = jnp.einsum(
        "qhtk,qthe->qkhe", d_cross_scores, cross_query, preferred_element_type=jnp.float32
    )
    d_all_keys = d_all_keys.reshape(questions, key_count, width)
    d_all_vals = d_all_vals.reshape(questions, key_count, width)
    d_enc_kv = jnp.concatenate([d_all_keys[:, top_count:], d_all_vals[:, top_count:]], axis=-1)
    d_enc_kv = d_enc_kv.astype(jnp.bfloat16).reshape(questions * enc_len, 2 * width)
    d_cross_kv = contract_rows(enc_flat, d_enc_kv)
    grad_encodings = (
        matmul_right_t(d_enc_kv, cross_kv).astype(jnp.bfloat16).reshape(questions, enc_len, width)
    )
    d_cross_q = contract_rows(normed_two, d_query)
    d_normed_two = matmul_right_t(d_query, cross_q)
    flat_ids = memory_ids.reshape(questions * top_count)
    d_mem_keys = (
        jnp.zeros((mem_rows, width), jnp.float32)
        .at[flat_ids]
        .add(d_all_keys[:, :top_count].reshape(questions * top_count, width))
    )
    d_mem_vals = (
        jnp.zeros((mem_rows, width), jnp.float32)
        .at[flat_ids]
        .add(d_all_vals[:, :top_count].reshape(questions * top_count, width))
    )
    d_back_two, d_gain_cross = norm_back(hidden_one, gain_cross, d_normed_two)
    grad_one = grad_two + d_back_two
    cr_a, cr_b, cr_c, cr_d, cr_e = (
        lax.psum_scatter(d_cross_q, "dp", scatter_dimension=0, tiled=True),
        lax.psum_scatter(d_cross_kv, "dp", scatter_dimension=0, tiled=True),
        lax.psum_scatter(d_cross_out, "dp", scatter_dimension=0, tiled=True),
        lax.psum_scatter(d_mem_keys, "dp", scatter_dimension=0, tiled=True),
        lax.psum_scatter(d_mem_vals, "dp", scatter_dimension=0, tiled=True),
    )
    sum_cross_q, sum_cross_kv, sum_cross_out, sum_mem_keys, sum_mem_vals = lax.psum(
        (cr_a, cr_b, cr_c, cr_d, cr_e), "replica"
    )
    branch_one = grad_one.astype(jnp.bfloat16)
    d_self_out = contract_rows(attended, branch_one)
    d_attended = (
        matmul_right_t(branch_one, self_out)
        .astype(jnp.bfloat16)
        .reshape(questions, length, heads, head_dim)
    )
    self_again = jnp.exp(self_scores() - self_lse)
    d_val_rows = jnp.einsum(
        "qhtu,qthe->quhe",
        self_again.astype(jnp.bfloat16),
        d_attended,
        preferred_element_type=jnp.float32,
    )
    d_self_probs = jnp.einsum(
        "qthe,quhe->qhtu", d_attended, val_rows, preferred_element_type=jnp.float32
    )
    self_delta = jnp.sum(self_again * d_self_probs, axis=-1, keepdims=True)
    d_self_scores = (self_again * (d_self_probs - self_delta)).astype(jnp.bfloat16)
    d_bias_cells = jnp.sum(d_self_scores.astype(jnp.float32), axis=0)
    d_rel_bias = jnp.einsum("tun,htu->nh", one_hot, d_bias_cells, precision=lax.Precision.HIGHEST)
    d_queries = jnp.einsum(
        "qhtu,quhe->qthe", d_self_scores, key_rows, preferred_element_type=jnp.float32
    )
    d_key_rows = jnp.einsum(
        "qhtu,qthe->quhe", d_self_scores, queries, preferred_element_type=jnp.float32
    )
    d_qkv = (
        jnp.stack([d_queries, d_key_rows, d_val_rows], axis=2)
        .astype(jnp.bfloat16)
        .reshape(token_rows, 3 * width)
    )
    d_self_qkv = contract_rows(normed_one, d_qkv)
    d_normed_one = matmul_right_t(d_qkv, self_qkv)
    d_back_one, d_gain_self = norm_back(tok_flat, gain_self, d_normed_one)
    grad_tokens = (grad_one + d_back_one).astype(jnp.bfloat16).reshape(questions, length, width)
    sf_a, sf_b = (
        lax.psum_scatter(d_self_qkv, "dp", scatter_dimension=0, tiled=True),
        lax.psum_scatter(d_self_out, "dp", scatter_dimension=0, tiled=True),
    )
    sum_self_qkv, sum_self_out = lax.psum((sf_a, sf_b), "replica")
    sum_rel_bias, all_gain_self, all_gain_cross, all_gain_ff = lax.psum(
        (d_rel_bias, d_gain_self, d_gain_cross, d_gain_ff), ("dp", "replica")
    )
    sum_gain_self = own_rows(all_gain_self)
    sum_gain_cross = own_rows(all_gain_cross)
    sum_gain_ff = own_rows(all_gain_ff)
    return (
        layer_output,
        grad_tokens,
        grad_encodings,
        sum_gain_self,
        sum_gain_cross,
        sum_gain_ff,
        sum_rel_bias,
        sum_self_qkv,
        sum_self_out,
        sum_cross_q,
        sum_cross_kv,
        sum_cross_out,
        sum_ff_in,
        sum_ff_out,
        sum_mem_keys,
        sum_mem_vals,
    )


def solution(mesh):
    placed = (
        P(("dp", "replica"), None, None),
        P(("dp", "replica"), None, None),
        P(("dp", "replica")),
        P(("dp", "replica"), None),
        P(),
        P(),
        P(),
        P(),
        P(),
        P(),
        P(),
        P(),
        P(),
        P(),
        P(),
        P(),
        P(),
        P(("dp", "replica"), None, None),
    )
    return jax.shard_map(
        on_device,
        mesh=mesh,
        in_specs=placed,
        out_specs=(
            P(("dp", "replica"), None, None),
            P(("dp", "replica"), None, None),
            P(("dp", "replica"), None, None),
            P("dp"),
            P("dp"),
            P("dp"),
            P(),
            P("dp", None),
            P("dp", None),
            P("dp", None),
            P("dp", None),
            P("dp", None),
            P("dp", None),
            P("dp", None),
            P("dp", None),
            P("dp", None),
        ),
        check_vma=False,
    )
```

profile of v0, /device:TPU:0, one launch (start us, length us, event | category | flops | bytes accessed | tf_op | source)
XLA Modules:
  0.0 892.4 jit_solution(7250465398102708056)
XLA Ops:
  14.5 3.5 convolution_convert_fusion.1
  17.9 4.3 copy.87
  22.2 5.3 reshape.285
  27.5 3.9 fusion.97
  32.9 60.0 %gather_fusion = f32[16384,12]{1,0:T(8,128)} fusion(f32[32,12]{1,0:T(8,128)S(1)} %copy.91, s32[16384]{0:T(1024)} %broadcast_clamp_fusion), kind=kCustom, calls=%fused_computation.2 | custom fusion | bytes 1638400 | tf_op jit(solution)/shard_map/gather | solution.py:95
  92.9 7.4 copy.92
  142.1 20.3 %multiply_convert_fusion = (bf16[512,3072]{1,0:T(8,128)(2,1)}, f32[512,3072]{1,0:T(8,128)}, f32[512,3072]{1,0:T(8,128)}) fusion(bf16[768,3072]{1,0:T(8,128)(2,1)} %param.36, f32[512,768]{1,0:T(8,128)S(1)} %get-tuple-element.104, f32[768]{0:T(1024)S(1)} %copy-done.48, f32[512]{0:T(512)S(1)} %fusion.87), kind=kOutput, calls=%fused_computation.16 | convolution fusion | flops 2519334912 | bytes 22025216 | tf_op jit(solution)/shard_map/dot_general | solution.py:43
  162.4 8.7 fusion.5
  171.2 3.4 multiply_reduce_fusion.2
  182.7 2.9 multiply_reduce_fusion.1
  198.7 4.2 convolution_bitcast_fusion
  202.9 6.1 copy.122
  215.0 3.9 fusion.45
  219.2 4.3 multiply_reduce_fusion.3
  227.4 3.4 convolution_convert_fusion.3
  235.6 4.0 multiply_reduce_fusion
  249.2 5.0 fusion.14
  254.9 9.2 %fusion.92 = f32[768,3072]{1,0:T(8,128)} fusion(bf16[512,3072]{1,0:T(8,128)(2,1)} %copy-done.32, f32[512,768]{1,0:T(8,128)} %copy-done.7, f32[768]{0:T(1024)S(1)} %copy-done.49, f32[512]{0:T(512)S(1)} %copy-done.52), kind=kOutput, calls=%fused_computation.181 | convolution fusion | flops 2417098752 | bytes 14160896 | tf_op jit(solution)/shard_map/dot_general | solution.py:47
  264.1 8.4 fusion.100
  277.5 2.6 copy.130
  287.6 24.3 %reduce-scatter.14.cloned.1.call-done = f32[96,768]{1,0:T(8,128)} async-done(((f32[768,768]{1,0:T(8,128)}), f32[96,768]{1,0:T(8,128)}) %reduce-scatter.14.cloned.1.call-update) | async-done | bytes 294928 | tf_op jit(solution)/shard_map/reduce_scatter | solution.py:227
  312.0 45.9 %reduce-scatter.16.cloned.1.call-done = f32[96,768]{1,0:T(8,128)} async-done(((f32[768,768]{1,0:T(8,128)}), f32[96,768]{1,0:T(8,128)}) %reduce-scatter.16.cloned.1.call-update) | async-done | bytes 294928 | tf_op jit(solution)/shard_map/reduce_scatter | solution.py:229
  357.9 46.1 %reduce-scatter.12.cloned.1.call-done = f32[96,768]{1,0:T(8,128)} async-done(((f32[768,768]{1,0:T(8,128)}), f32[96,768]{1,0:T(8,128)}) %reduce-scatter.12.cloned.1.call-update) | async-done | bytes 294928 | tf_op jit(solution)/shard_map/reduce_scatter | solution.py:274
  404.0 68.9 %reduce-scatter.10.cloned.1.call-done = f32[96,2304]{1,0:T(8,128)} async-done(((f32[768,2304]{1,0:T(8,128)}), f32[96,2304]{1,0:T(8,128)}) %reduce-scatter.10.cloned.1.call-update) | async-done | bytes 884752 | tf_op jit(solution)/shard_map/reduce_scatter | solution.py:273
  472.9 80.3 %reduce-scatter.18.cloned.1.call-done = f32[96,3072]{1,0:T(8,128)} async-done(((f32[768,3072]{1,0:T(8,128)}), f32[96,3072]{1,0:T(8,128)}) %reduce-scatter.18.cloned.1.call-update) | async-done | bytes 1179664 | tf_op jit(solution)/shard_map/reduce_scatter | solution.py:173
  553.1 80.4 %reduce-scatter.20.cloned.1.call-done = f32[384,768]{1,0:T(8,128)} async-done(((f32[3072,768]{1,0:T(8,128)}), f32[384,768]{1,0:T(8,128)}) %reduce-scatter.20.cloned.1.call-update) | async-done | bytes 1179664 | tf_op jit(solution)/shard_map/reduce_scatter | solution.py:174
  638.5 5.9 fusion.30
  644.4 40.2 %all-reduce.2 = (f32[768]{0:T(1024)}, f32[768]{0:T(1024)}, f32[768]{0:T(1024)}, f32[32,12]{0,1:T(8,128)}) all-reduce(f32[768]{0:T(1024)} %get-tuple-element.69, f32[768]{0:T(1024)} %get-tuple-element.67, f32[768]{0:T(1024)} %get-tuple-element.65, f32[32,12]{0,1:T(8,128)S(1)} %fusion.39), channel_id=1, replica_groups=mesh['dp'=8,'replica'=4] {'dp','replica'}, use_global_device_ids=true, to_apply=%region_13.15 | all-reduce | flops 2688 | bytes 21504 | tf_op jit(solution)/shard_map/psum | solution.py:277
  691.2 3.9 convolution_convert_fusion.9
  697.7 6.2 select_convert_fusion
  706.0 21.7 %all-reduce.4 = (f32[4,768]{1,0:T(4,128)}, f32[4,768]{1,0:T(4,128)}) all-reduce(f32[4,768]{1,0:T(4,128)} %constant_dynamic-slice_fusion.1, f32[4,768]{1,0:T(4,128)S(1)} %constant_dynamic-slice_fusion), channel_id=1, replica_groups=mesh['dp'=8,'replica'=4] {'replica'}, use_global_device_ids=true, to_apply=%region_36.38 | all-reduce | flops 6144 | bytes 49152 | tf_op jit(solution)/shard_map/psum | solution.py:233
  727.7 148.0 %all-reduce.11.cloned.1.call-done = (f32[96,2304]{1,0:T(8,128)}, f32[96,768]{1,0:T(8,128)}, f32[96,768]{1,0:T(8,128)}, f32[96,1536]{0,1:T(8,128)}, f32[96,768]{1...) async-done(((f32[96,2304]{1,0:T(8,128)}, f32[96,768]{1,0:T(8,128)}, f32[96,768]{1,0:T(8,128)}, f32[96,1536]{0,1:T(8,128)}, f32[96,768]{1,0:T(8,128)}, ...) | async-done | bytes 4718608 | tf_op jit(solution)/shard_map/psum | solution.py:276
  (265 shorter events, 134.2 us)
Async XLA Ops:
  7.2 7.3 copy-start
  7.2 278.2 %reduce-scatter.22.cloned.1.call-start = ((), (), s32[]{:S(2)}) async-start(), calls=%async_computation.13 | async-start | bytes 5308416
  92.8 7.4 copy-start.42
  140.5 30.7 %slice-start = ((s8[4718592]{0:T(1024)(128)(4,1)}), s8[4194304]{0:T(1024)(128)(4,1)S(1)}, s32[]{:S(2)}) async-start(s8[4718592]{0:T(1024)(128)(4,1)} %bitcast.209), calls=%async_computation.16 | async-start | bytes 8388608
  141.5 33.1 %copy-start.7 = (f32[512,768]{1,0:T(8,128)}, f32[512,768]{1,0:T(8,128)S(1)}, u32[]{:S(2)}) copy-start(f32[512,768]{1,0:T(8,128)S(1)} %get-tuple-element.104) | copy-start | bytes 4718596
  141.5 33.1 %copy-start.51 = (f32[512]{0:T(512)}, f32[512]{0:T(512)S(1)}, u32[]{:S(2)}) copy-start(f32[512]{0:T(512)S(1)} %fusion.87) | copy-start | bytes 6148
  141.9 32.7 %copy-start.66 = (pred[512]{0:T(512)(128)(4,1)}, pred[512]{0:T(512)(128)(4,1)S(1)}, u32[]{:S(2)}) copy-start(pred[512]{0:T(512)(128)(4,1)S(1)} %fusion.85) | copy-start | bytes 1540
  142.1 20.3 %copy-start.43 = (bf16[512,768]{1,0:T(8,128)(2,1)}, bf16[512,768]{1,0:T(8,128)(2,1)S(1)}, u32[]{:S(2)}) copy-start(bf16[512,768]{1,0:T(8,128)(2,1)S(1)} %fusion.26) | copy-start | bytes 2359300
  142.1 29.0 %slice-start.1 = ((s8[4718592]{0:T(1024)(128)(4,1)}), s8[524288]{0:T(1024)(128)(4,1)S(1)}, s32[]{:S(2)}) async-start(s8[4718592]{0:T(1024)(128)(4,1)} %bitcast.209), calls=%async_computation.17 | async-start | bytes 1048576
  209.0 102.9 %reduce-scatter.14.cloned.1.call-start = ((), (), s32[]{:S(2)}) async-start(), calls=%async_computation.9 | async-start | bytes 2654208 | tf_op jit(solution)/shard_map/reduce_scatter | solution.py:227
  215.0 142.9 %reduce-scatter.16.cloned.1.call-start = ((), (), s32[]{:S(2)}) async-start(), calls=%async_computation.10 | async-start | bytes 2654208 | tf_op jit(solution)/shard_map/reduce_scatter | solution.py:229
  218.9 185.0 %reduce-scatter.12.cloned.1.call-start = ((), (), s32[]{:S(2)}) async-start(), calls=%async_computation.8 | async-start | bytes 2654208 | tf_op jit(solution)/shard_map/reduce_scatter | solution.py:274
  219.1 4.3 copy-start.65
  219.1 4.3 copy-start.12
  219.2 4.3 copy-start.16
  219.2 4.3 copy-start.58
  219.2 4.3 copy-start.63
  227.3 245.6 %reduce-scatter.10.cloned.1.call-start = ((), (), s32[]{:S(2)}) async-start(), calls=%async_computation.7 | async-start | bytes 7962624 | tf_op jit(solution)/shard_map/reduce_scatter | solution.py:273
  235.6 4.0 copy-start.2
  235.6 4.0 copy-start.6
  235.6 4.0 copy-start.40
  254.2 298.9 %reduce-scatter.18.cloned.1.call-start = ((), (), s32[]{:S(2)}) async-start(), calls=%async_computation.11 | async-start | bytes 10616832 | tf_op jit(solution)/shard_map/reduce_scatter | solution.py:173
  264.1 369.4 %reduce-scatter.20.cloned.1.call-start = ((), (), s32[]{:S(2)}) async-start(), calls=%async_computation.12 | async-start | bytes 10616832 | tf_op jit(solution)/shard_map/reduce_scatter | solution.py:174
  272.5 431.4 %all-reduce.9.cloned.1.call-start = ((), (), s32[]{:S(2)}) async-start(), calls=%async_computation.14 | async-start | bytes 393216
  285.3 590.4 %all-reduce.11.cloned.1.call-start = ((), (), s32[]{:S(2)}) async-start(), calls=%async_computation.15 | async-start | bytes 9830400 | tf_op jit(solution)/shard_map/psum | solution.py:276
  690.3 4.7 copy-start.14
  690.3 4.7 copy-start.19
  690.3 4.7 copy-start.35
  877.9 4.1 copy-start.47
  877.9 4.8 copy-start.46
  877.9 5.5 copy-start.37
  880.2 4.2 copy-start.36
  (52 other events, 97.0 us)
Sparse Core Ops, SparseCore 0:
  209.2 56.5 reduce-scatter.21
  269.5 42.4 reduce-scatter.13
  315.3 42.5 reduce-scatter.15
  361.5 42.4 reduce-scatter.11
  407.3 65.5 reduce-scatter.9
  476.6 76.4 reduce-scatter.17
  557.0 76.4 reduce-scatter.19
  637.5 53.4 all-reduce.8
  694.8 180.8 all-reduce.10
where the time goes:
time: 904 us; the launch traced here: 892 us
  waiting for transfers between devices  494 us (55%)
  local copies, waits for them, and re-layouts  171 us (19%)
  matrix products  127 us (14%)
  blocking collectives  61.9 us (7%)
  other arithmetic  22.1 us (2%)
  between operations  15.9 us (2%)
    psum x1, waiting for transfers between devices, on_device(): sum_self_qkv, sum_self_out = lax.psum((sf_a, sf_b), 'replica')  148 us
    reduce_scatter x1, waiting for transfers between devices, on_device(): lax.psum_scatter(d_ff_out, 'dp', scatter_dimension=0, tiled=True)  80.4 us
    reduce_scatter x1, waiting for transfers between devices, on_device(): lax.psum_scatter(d_ff_in, 'dp', scatter_dimension=0, tiled=True)  80.3 us
    reduce_scatter x1, waiting for transfers between devices, on_device(): lax.psum_scatter(d_self_qkv, 'dp', scatter_dimension=0, tiled=True)  68.9 us
    gather x2, local copies, waits for them, and re-layouts, on_device(): pos_bias = jnp.transpose(rel_bias[buckets], (2, 0, 1))  67.4 us
    reduce_scatter x1, waiting for transfers between devices, on_device(): lax.psum_scatter(d_self_out, 'dp', scatter_dimension=0, tiled=True)  46.1 us
    reduce_scatter x1, waiting for transfers between devices, on_device(): lax.psum_scatter(d_cross_out, 'dp', scatter_dimension=0, tiled=True)  45.9 us
    unnamed x167, local copies, waits for them, and re-layouts  44.9 us
  transfers between devices with their start and end apart: 9, of which 7 were waited for; matrix products, arithmetic and copies ran while one was open for 12% of the time, Pallas kernels for 0%

commit v1 on v0

v1 whole, which is shorter than its diff:
```python
import functools
from types import SimpleNamespace as Bunch

import jax
import jax.numpy as jnp
import numpy as np
from jax import lax
from jax.experimental import pallas as pl
from jax.experimental.pallas import tpu as pltpu
from jax.sharding import PartitionSpec as P

F32, BF16 = jnp.float32, jnp.bfloat16
EPSILON = 1e-06
NEGATIVE = -1000000000.0
MAXDIST = 128
LANES = 128
E3, B2, CQ, EKV, B1, QKV, RIGHT = 0, 768, 1536, 2304, 3840, 4608, 6912
L_H3, L_O2, L_H2, L_ENC, L_O, L_H1, L_R = 0, 1, 2, 3, 4, 5, 6
FF_TILE = 384
MEM_PAD = 16


def nn(a, b, **kw):
    return lax.dot_general(a, b, (((1,), (0,)), ((), ())), preferred_element_type=F32, **kw)


def nt(a, b, **kw):
    return lax.dot_general(a, b, (((1,), (1,)), ((), ())), preferred_element_type=F32, **kw)


def tn(a, b, **kw):
    return lax.dot_general(a, b, (((0,), (0,)), ((), ())), preferred_element_type=F32, **kw)


def bucket_of(apart, buckets, distance):
    exact = buckets // 2
    spread = np.log(np.maximum(apart, 1) / exact) / np.log(distance / exact) * (buckets - exact)
    larger = np.minimum(exact + np.floor(np.maximum(spread, 0.0)).astype(np.int64), buckets - 1)
    return np.where(apart < exact, apart, larger).astype(np.int32)


def bucket_tables(length, buckets):
    lane = np.arange(length)
    spread = [bucket_of((length - lane) % length, buckets, MAXDIST), bucket_of(length - 1 - lane, buckets, MAXDIST)]
    return np.stack([(np.arange(buckets)[:, None] == row[None]).astype(np.float32) for row in spread])


def root_scale(v):
    return lax.rsqrt(jnp.mean(v * v, axis=-1, keepdims=True) + EPSILON)


def normed(v, gain):
    return (v * root_scale(v) * gain).astype(BF16)


def norm_pull(v, gain, w):
    scale = root_scale(v)
    gw = w * gain
    back = scale * gw - v * (scale * scale * scale) * jnp.mean(gw * v, axis=-1, keepdims=True)
    return back, jnp.sum(w * v * scale, axis=0, keepdims=True)


def head_masks():
    lane = lax.broadcasted_iota(jnp.int32, (1, LANES), 1)
    first = jnp.where(lane < LANES // 2, 1.0, 0.0)
    return first.astype(BF16), (1.0 - first).astype(BF16), first > 0.5


def stacked(rows, m0, m1):
    return jnp.concatenate([rows * m0, rows * m1], axis=0)


def pair_softmax(s):
    parts = []
    for part in (s[:, :LANES], s[:, LANES:]):
        e = jnp.exp(part - jnp.max(part, axis=-1, keepdims=True))
        parts.append(e * (1.0 / jnp.sum(e, axis=-1, keepdims=True)))
    return jnp.concatenate(parts, axis=1)


def pair_pull(p, dp):
    parts = []
    for lo in (0, LANES):
        a, b = p[:, lo:lo + LANES], dp[:, lo:lo + LANES]
        parts.append((a * (b - jnp.sum(a * b, axis=-1, keepdims=True))).astype(BF16))
    return jnp.concatenate(parts, axis=1)


class Layer:
    def __init__(self, given, hbm, out, vm, load, store):
        vars(self).update(vars(given))
        vars(self).update(vars(vm))
        self.hbm, self.out, self.store = hbm, out, store
        self.questions, self.length, self.enc_len = 4, 128, 64
        self.rows = self.questions * self.length
        self.load = Bunch(**{name: pltpu.make_async_copy(vars(hbm)[name], vars(vm)[name], sem)
                             for name, sem in vars(load).items()})

    def ff_loads(self, j):
        slot = lax.rem(j, 2)
        at = pl.ds(pl.multiple_of(j * FF_TILE, FF_TILE), FF_TILE)
        return (
            pltpu.make_async_copy(self.hbm.ff_in.at[:, at], self.wi.at[slot], self.wi_sem.at[slot]),
            pltpu.make_async_copy(self.hbm.ff_out.at[at, :], self.wo.at[slot], self.wo_sem.at[slot]),
        )

    def q_rows(self, q, n=128):
        return pl.ds(pl.multiple_of(q * n, n), n)

    def put_left(self, index, q, rows):
        turned = rows.T
        width = turned.shape[1]
        at = self.q_rows(q, width)
        for b in range(8):
            self.left[index, b % 2, (b // 2) * 96:(b // 2 + 1) * 96, at] = turned[b * 96:(b + 1) * 96]

    def bias_tables(self):
        table = nn(self.rel_bias[...], self.tables[0], precision=lax.Precision.HIGHEST)
        for p in range(6):
            for k in range(2):
                row = table[2 * p + k:2 * p + k + 1, :]
                self.bias[p, :, k * LANES:(k + 1) * LANES] = pltpu.roll(
                    jnp.broadcast_to(row, (LANES, LANES)), 0, 1, stride=1, stride_axis=0)

    def memory_rows(self):
        entries = self.memory_keys.shape[0]
        slot = lax.broadcasted_iota(jnp.int32, (MEM_PAD, entries), 0)
        entry = lax.broadcasted_iota(jnp.int32, (MEM_PAD, entries), 1)
        for q in range(self.questions):
            wanted = jnp.full((MEM_PAD, entries), -1, jnp.int32)
            for i in range(self.ids.shape[1]):
                wanted = jnp.where(slot == i, self.ids[q, i], wanted)
            pick = jnp.where(wanted == entry, 1.0, 0.0).astype(BF16)
            self.mem_k[q] = nn(pick, self.memory_keys[...]).astype(BF16)
            self.mem_v[q] = nn(pick, self.memory_values[...]).astype(BF16)

    def causal(self):
        row = lax.broadcasted_iota(jnp.int32, (LANES, 2 * LANES), 0)
        col = lax.rem(lax.broadcasted_iota(jnp.int32, (LANES, 2 * LANES), 1), LANES)
        return col <= row

    def self_probs(self, q2, k2, p, allowed):
        return pair_softmax(jnp.where(allowed, nt(q2, k2) + self.bias[p], NEGATIVE))

    def cross_probs(self, q2, k2, present):
        return pair_softmax(jnp.where(present, nt(q2, k2), -1e30))

    def present(self):
        col = lax.rem(lax.broadcasted_iota(jnp.int32, (1, 2 * LANES), 1), LANES)
        return col < self.enc_len + self.ids.shape[1]

    def cross_side(self, q, p, memory, base):
        enc = self.right[self.q_rows(q, self.enc_len), base + p * LANES:base + (p + 1) * LANES]
        mem = memory[q, :, p * LANES:(p + 1) * LANES]
        return jnp.concatenate([enc, mem, jnp.zeros((LANES - 64 - MEM_PAD, LANES), BF16)], axis=0)

    def forward(self, enter):
        load = self.load
        for copy in (load.tokens, load.self_qkv, load.encodings, load.cross_kv, load.memory_keys, load.memory_values,
                     load.self_out, load.cross_q, load.cross_out):
            copy.start()
        for copy in self.ff_loads(0) + self.ff_loads(1):
            copy.start()
        load.cotangent.start()
        enter()
        for n, gain in enumerate((self.gain_self, self.gain_cross, self.gain_ff)):
            self.gains[n:n + 1, :] = gain[...].reshape(1, gain.shape[0])
        right = self.right
        self.bias_tables()
        self.load.tokens.wait()

        def norm_one(q, c):
            at = self.q_rows(q)
            self.hid[at] = normed(self.tokens[at].astype(F32), self.gains[0:1])
            return c
        lax.fori_loop(0, 4, norm_one, 0)
        self.load.self_qkv.wait()

        def qkv_tile(j, c):
            at = self.q_rows(j, 256)
            right[:, pl.ds(pl.multiple_of(QKV + j * 256, 256), 256)] = nn(self.hid[...], self.self_qkv[:, at]).astype(BF16)
            return c
        lax.fori_loop(0, 9, qkv_tile, 0)

        m0, m1, _ = head_masks()
        allowed = self.causal()

        def self_attention(q, c):
            at = self.q_rows(q)
            for p in range(6):
                lo = p * LANES
                q2, k2, v2 = (right[at, QKV + 768 * i + lo:QKV + 768 * i + lo + LANES] for i in range(3))
                probs = self.self_probs(q2, stacked(k2, m0, m1), p, allowed).astype(BF16)
                self.att[at, lo:lo + LANES] = nn(probs, stacked(v2, m0, m1)).astype(BF16)
            return c
        lax.fori_loop(0, 4, self_attention, 0)

        self.load.encodings.wait()
        self.load.cross_kv.wait()
        enc_rows = self.questions * self.enc_len

        def ekv_tile(j, c):
            at = self.q_rows(j, 256)
            col = pl.ds(pl.multiple_of(EKV + j * 256, 256), 256)
            right[0:enc_rows, col] = nn(self.encodings[...], self.cross_kv[:, at]).astype(BF16)
            return c
        lax.fori_loop(0, 6, ekv_tile, 0)
        self.load.memory_keys.wait()
        self.load.memory_values.wait()
        self.memory_rows()
        self.load.self_out.wait()

        def out_tile(j, c):
            at = self.q_rows(j, 256)
            self.y1[:, at] = self.tokens[:, at].astype(F32) + nn(self.att[...], self.self_out[:, at])
            return c
        lax.fori_loop(0, 3, out_tile, 0)

        def norm_two(q, c):
            at = self.q_rows(q)
            self.hid[at] = normed(self.y1[at], self.gains[1:2])
            return c
        lax.fori_loop(0, 4, norm_two, 0)
        self.load.cross_q.wait()

        def cq_tile(j, c):
            at = self.q_rows(j, 256)
            right[:, pl.ds(pl.multiple_of(CQ + j * 256, 256), 256)] = nn(self.hid[...], self.cross_q[:, at]).astype(BF16)
            return c
        lax.fori_loop(0, 3, cq_tile, 0)
        present = self.present()

        def cross_attention(q, c):
            at = self.q_rows(q)
            for p in range(6):
                lo = p * LANES
                keys = self.cross_side(q, p, self.mem_k, EKV)
                vals = self.cross_side(q, p, self.mem_v, EKV + 768)
                probs = self.cross_probs(right[at, CQ + lo:CQ + lo + LANES], stacked(keys, m0, m1), present)
                self.att2[at, lo:lo + LANES] = nn(probs.astype(BF16), stacked(vals, m0, m1)).astype(BF16)
            return c
        lax.fori_loop(0, 4, cross_attention, 0)
        self.load.cross_out.wait()

        def out2_tile(j, c):
            at = self.q_rows(j, 256)
            self.y2[:, at] = self.y1[:, at] + nn(self.att2[...], self.cross_out[:, at])
            return c
        lax.fori_loop(0, 3, out2_tile, 0)
        self.load.cotangent.wait()

        def norm_three(q, c):
            at = self.q_rows(q)
            h3 = normed(self.y2[at], self.gains[2:3])
            self.hid[at] = h3
            self.put_left(L_H3, q, h3)
            valid = lax.broadcasted_iota(jnp.int32, (LANES, 1), 0) < self.lengths[q]
            cot = jnp.where(valid, self.cotangent[at].astype(F32), 0.0)
            right[at, E3:E3 + 768] = cot.astype(BF16)
            return c
        lax.fori_loop(0, 4, norm_three, 0)

    def feed_forward(self):
        right = self.right
        self.y3[...] = self.y2[...]
        self.dh3[...] = jnp.zeros_like(self.dh3)

        def tile(j, c):
            slot = lax.rem(j, 2)
            for copy in self.ff_loads(j):
                copy.wait()
            self.z[...] = nn(self.hid[...], self.wi[slot])
            self.dr[...] = nt(right[:, E3:E3 + 768], self.wo[slot])

            def gelu(i, c):
                at = pl.ds(pl.multiple_of(i * 32, 32), 32)
                z = self.z[at]
                cdf = 0.5 * (1.0 + lax.erf(z * 0.7071067811865476))
                pdf = jnp.exp(-0.5 * z * z) * 0.3989422804014327
                self.act[at] = (z * cdf).astype(BF16)
                dr = self.dr[at].astype(BF16).astype(F32)
                self.dz[at] = (dr * (cdf + z * pdf)).astype(BF16)
                return c
            lax.fori_loop(0, 16, gelu, 0)

            act = self.act[...]
            dz = self.dz[...]

            self.advance(j, 0, lambda: dz)
            turned = act.T
            for g in range(4):
                at = pl.ds(pl.multiple_of((j // 2) * 96, 96), 96)
                self.left[L_R + g, lax.rem(j, 2), at, :] = turned[g * 96:(g + 1) * 96]
            for n in range(3):
                at = slice(n * 256, (n + 1) * 256)
                self.y3[:, at] += nn(act, self.wo[slot][:, at])
                self.dh3[:, at] += nt(dz, self.wi[slot][at])

            @pl.when(j + 2 < 8)
            def _():
                for copy in self.ff_loads(j + 2):
                    copy.start()
            return c
        lax.fori_loop(0, 8, tile, 0)

        def finish(q, c):
            at = self.q_rows(q)
            valid = lax.broadcasted_iota(jnp.int32, (LANES, 1), 0) < self.lengths[q]
            self.layer_output[at] = jnp.where(valid, self.y3[at], 0.0).astype(BF16)
            return c
        lax.fori_loop(0, 4, finish, 0)
        self.stores()[0].start()

    def stores(self):
        return [pltpu.make_async_copy(vars(self)[name], vars(self.out)[name], sem) for name, sem in vars(self.store).items()]

    def backward_cross(self):
        right = self.right
        m0, m1, low_lanes = head_masks()
        present = self.present()
        enc_rows = self.questions * self.enc_len
        self.dgains[...] = jnp.zeros_like(self.dgains)
        self.left[L_ENC, :, :, enc_rows:] = jnp.zeros((2, 384, self.rows - enc_rows), BF16)
        turned = self.encodings[...].T
        for b in range(8):
            self.left[L_ENC, b % 2, (b // 2) * 96:(b // 2 + 1) * 96, 0:enc_rows] = turned[b * 96:(b + 1) * 96]
        right[enc_rows:, EKV:EKV + 1536] = jnp.zeros((self.rows - enc_rows, 1536), BF16)

        def pick(both):
            return jnp.where(low_lanes, both[:LANES], both[LANES:])

        def question(q, c):
            at = self.q_rows(q)
            enc_at = self.q_rows(q, self.enc_len)
            mem_at = self.q_rows(q, MEM_PAD)
            back, gain = norm_pull(self.y2[at], self.gains[2:3], self.dh3[at])
            self.dgains[2:3] += gain
            e2 = right[at, E3:E3 + 768].astype(F32) + back
            self.y3[at] = e2
            b2 = e2.astype(BF16)
            right[at, B2:B2 + 768] = b2
            self.up[...] = nt(b2, self.cross_out[...]).astype(BF16)
            for p in range(6):
                lo = p * LANES
                pair = slice(lo, lo + LANES)
                keys = stacked(self.cross_side(q, p, self.mem_k, EKV), m0, m1)
                vals = stacked(self.cross_side(q, p, self.mem_v, EKV + 768), m0, m1)
                cq = right[at, CQ + lo:CQ + lo + LANES]
                probs = self.cross_probs(cq, keys, present)
                up = self.up[:, pair]
                dvals = pick(tn(probs.astype(BF16), up))
                ds = pair_pull(probs, nt(up, vals))
                dkeys = pick(tn(ds, cq))
                right[at, CQ + lo:CQ + lo + LANES] = nn(ds, keys).astype(BF16)
                right[enc_at, EKV + lo:EKV + lo + LANES] = dkeys[:64].astype(BF16)
                right[enc_at, EKV + 768 + lo:EKV + 768 + lo + LANES] = dvals[:64].astype(BF16)
                self.dmem_k[mem_at, pair] = dkeys[64:64 + MEM_PAD]
                self.dmem_v[mem_at, pair] = dvals[64:64 + MEM_PAD]
                if p == 2:
                    self.advance(8 + 2 * q)
            self.grad_encodings[enc_at] = nt(right[enc_at, EKV:EKV + 1536], self.cross_kv[...]).astype(BF16)
            y1 = self.y1[at]
            back, gain = norm_pull(y1, self.gains[1:2], nt(right[at, CQ:CQ + 768], self.cross_q[...]))
            self.dgains[1:2] += gain
            self.y3[at] += back
            self.put_left(L_H2, q, normed(y1, self.gains[1:2]))
            self.put_left(L_O2, q, self.att2[at])
            self.advance(9 + 2 * q)
            return c
        lax.fori_loop(0, 4, question, 0)

    def backward_self(self):
        right = self.right
        m0, m1, low_lanes = head_masks()
        allowed = self.causal()
        self.dbias[...] = jnp.zeros_like(self.dbias)

        def pick(both):
            return jnp.where(low_lanes, both[:LANES], both[LANES:])

        def question(q, c):
            at = self.q_rows(q)
            b1 = self.y3[at].astype(BF16)
            right[at, B1:B1 + 768] = b1
            self.up[...] = nt(b1, self.self_out[...]).astype(BF16)
            for p in range(6):
                lo = p * LANES
                pair = slice(lo, lo + LANES)
                q2, k2, v2 = (right[at, QKV + 768 * i + lo:QKV + 768 * i + lo + LANES] for i in range(3))
                keys = stacked(k2, m0, m1)
                probs = self.self_probs(q2, keys, p, allowed)
                up = self.up[:, pair]
                dval = pick(tn(probs.astype(BF16), up))
                ds = pair_pull(probs, nt(up, stacked(v2, m0, m1)))
                self.dbias[p] += ds.astype(F32)
                right[at, QKV + lo:QKV + lo + LANES] = nn(ds, keys).astype(BF16)
                right[at, QKV + 768 + lo:QKV + 768 + lo + LANES] = pick(tn(ds, q2)).astype(BF16)
                right[at, QKV + 1536 + lo:QKV + 1536 + lo + LANES] = dval.astype(BF16)
                if p == 2:
                    self.advance(16 + 2 * q)
            tok = self.tokens[at].astype(F32)
            back, gain = norm_pull(tok, self.gains[0:1], nt(right[at, QKV:QKV + 2304], self.self_qkv[...]))
            self.dgains[0:1] += gain
            self.grad_tokens[at] = (self.y3[at] + back).astype(BF16)
            self.put_left(L_H1, q, normed(tok, self.gains[0:1]))
            self.put_left(L_O, q, self.att[at])
            self.advance(17 + 2 * q)
            return c
        lax.fori_loop(0, 4, question, 0)
        for copy in self.stores()[1:]:
            copy.start()

    def bias_rows(self):
        row = lax.broadcasted_iota(jnp.int32, (LANES, LANES), 0)
        col = lax.broadcasted_iota(jnp.int32, (LANES, LANES), 1)
        flip = jnp.where(row + col == LANES - 1, 1.0, 0.0)
        out = []
        for p in range(6):
            turned = nn(flip, self.dbias[p], precision=lax.Precision.HIGHEST)
            for k in range(2):
                rolled = pltpu.roll(turned[:, k * LANES:(k + 1) * LANES], 0, 1, stride=1, stride_axis=0)
                out.append(jnp.sum(rolled, axis=0, keepdims=True))
        return out

    def spread_ids(self, width):
        slot = lax.broadcasted_iota(jnp.int32, (4 * MEM_PAD, width), 0)
        wanted = jnp.full((4 * MEM_PAD, width), -1, jnp.int32)
        for q in range(self.questions):
            for i in range(self.ids.shape[1]):
                wanted = jnp.where(slot == q * MEM_PAD + i, self.ids[q, i], wanted)
        return wanted

    def advance(self, t, fixed=None, right=None):
        left, value = self.place(t)
        if fixed is not None:
            left, value = fixed, right

        def product(parity):
            return nn(self.left[left, parity], value())
        self.reducer.step(t, product)

    def place(self, d):
        u = d - 16
        late = jnp.where(u < 4, 1 + u // 2, jnp.where(u < 8, 3, jnp.where(u < 10, 4, 5)))
        left = jnp.where(d < 16, L_R + (d - 8) // 2, late)
        col = pl.multiple_of(jnp.where(d < 16, E3 + lax.rem(d, 2) * 384, B2 + u * 384), LANES)
        return left, lambda: self.right[:, pl.ds(col, 384)]


MESH_ID = pl.DeviceIdType.MESH
CHUNK_ROWS, CHUNK_COLS, PAIR_ROWS, SMALL_ROWS = 96, 384, 48, 32
PERIOD, GAP, LAST_PAIR, SMALL_AT = 5, 31, 26, 33
CHUNKS = 32
DEPTH = Bunch(own=12, mid=8, snd=3, r0=3, rp=2, r1=4, r2=4, r3=4, r4=4)
LAG = Bunch(one=1, two=2, three=2, four=2, five=2, six=2)
TAIL = sum(vars(LAG).values())


def number_of(d):
    if d == CHUNKS - 1:
        return GAP + 1
    return d + PERIOD if d % PERIOD == 1 else d


class Reducer:
    def __init__(self, bufs, sems, out_ref):
        self.b, self.s, self.out = bufs, sems, out_ref
        dp, z = lax.axis_index("dp"), lax.axis_index("replica")
        here = Bunch(dp=dp, replica=z)
        self.core = lax.rem(dp, 2)
        self.x = lax.rem(dp // 2, 2)
        self.y = dp // 4
        self.inner = lax.rem((z + 1) // 2, 2) == 1
        self.end = lax.rem((z + 1) // 2, 2) == 0
        self.near = pl.multiple_of(PAIR_ROWS * lax.rem(z, 2), PAIR_ROWS)
        self.far = pl.multiple_of(PAIR_ROWS * (1 - lax.rem(z, 2)), PAIR_ROWS)
        self.to_core = dict(vars(here), dp=dp + 1 - 2 * self.core)
        self.to_x = dict(vars(here), dp=dp + 2 - 4 * self.x)
        self.to_y = dict(vars(here), dp=dp + 4 - 8 * self.y)
        self.to_pair = dict(vars(here), replica=z + 1 - 2 * lax.rem(z, 2))
        self.to_mid = dict(vars(here), replica=3 - z)

    def enter(self):
        bar = pltpu.get_barrier_semaphore()
        for target in (self.to_core, self.to_x, self.to_y, self.to_pair, self.to_mid):
            pl.semaphore_signal(bar, inc=1, device_id=target, device_id_type=MESH_ID)
        pl.semaphore_wait(bar, 5)

    def copy(self, src, dst, send, recv, target):
        return pltpu.make_async_remote_copy(
            src_ref=src, dst_ref=dst, send_sem=send, recv_sem=recv, device_id=target, device_id_type=MESH_ID)

    def core_copy(self, k, n):
        a, r, rows = lax.rem(k, DEPTH.snd), lax.rem(k, DEPTH.r0), pl.ds(0, n)
        return self.copy(self.b.snd.at[a, :, rows], self.b.r0.at[r, :, rows], self.s.snd.at[a], self.s.r0.at[r],
                         self.to_core)

    def pair_copy(self, d):
        o, r = lax.rem(d + PERIOD, DEPTH.own), lax.rem(d // PERIOD, DEPTH.rp)
        return self.copy(self.b.own.at[o, :, :, pl.ds(self.far, PAIR_ROWS)], self.b.rp.at[r], self.s.sp.at[r],
                         self.s.rp.at[r], self.to_pair)

    def first_copies(self, k, n, base):
        o, r = lax.rem(k, DEPTH.own), lax.rem(k, DEPTH.r1)
        half = n // 2
        low, high, into = pl.ds(base, half), pl.ds(base + half, half), pl.ds(0, half)
        return (
            self.copy(self.b.own.at[o, :, 1 - self.x, low], self.b.r1x.at[r, :, into], self.s.s1x.at[r],
                      self.s.r1x.at[r], self.to_x),
            self.copy(self.b.own.at[o, 1 - self.y, :, high], self.b.r1y.at[r, :, into], self.s.s1y.at[r],
                      self.s.r1y.at[r], self.to_y),
        )

    def second_copies(self, k, n, base):
        o, r = lax.rem(k, DEPTH.own), lax.rem(k, DEPTH.r2)
        half = n // 2
        low, high, into = pl.ds(base, half), pl.ds(base + half, half), pl.ds(0, half)
        return (
            self.copy(self.b.own.at[o, self.y, 1 - self.x, high], self.b.r2x.at[r, into], self.s.s2x.at[r],
                      self.s.r2x.at[r], self.to_x),
            self.copy(self.b.own.at[o, 1 - self.y, self.x, low], self.b.r2y.at[r, into], self.s.s2y.at[r],
                      self.s.r2y.at[r], self.to_y),
        )

    def mine(self, k, n, base=0):
        return self.b.mid.at[lax.rem(k, DEPTH.mid), pl.ds(base, n)]

    def inward_copy(self, k, n, base):
        r = lax.rem(k, DEPTH.r3)
        return self.copy(self.mine(k, n, base), self.b.r3.at[r, pl.ds(0, n)], self.s.s3.at[r], self.s.r3.at[r],
                         self.to_pair)

    def middle_copy(self, k, n):
        r = lax.rem(k, DEPTH.r4)
        return self.copy(self.mine(k, n), self.b.r4.at[r, pl.ds(0, n)], self.s.s4.at[r], self.s.r4.at[r], self.to_mid)

    def outward_copy(self, k, n):
        r = lax.rem(k, DEPTH.r4)
        return self.copy(self.mine(k, n), self.out.at[k, pl.ds(0, n)], self.s.s5.at[r], self.s.out.at[k], self.to_pair)

    def keep_copy(self, k, n):
        return pltpu.make_async_copy(self.mine(k, n), self.out.at[k, pl.ds(0, n)], self.s.out.at[k])

    def grant(self, sem, k, depth, target):
        @pl.when(k + depth <= SMALL_AT)
        def _():
            pl.semaphore_signal(sem, inc=1, device_id=target, device_id_type=MESH_ID)

    def need(self, sem, k, depth):
        @pl.when((k >= depth) & (k != depth + 1))
        def _():
            pl.semaphore_wait(sem, 1)

    def fill(self, t, half_product):
        n = CHUNK_ROWS
        early = (lax.rem(t, PERIOD) == 1) & (t <= LAST_PAIR)
        a, o = lax.rem(t, DEPTH.snd), lax.rem(jnp.where(early, t + PERIOD, t), DEPTH.own)

        @pl.when(t >= DEPTH.snd)
        def _():
            self.core_copy(t - DEPTH.snd, n).wait_send()

        away = half_product(1 - self.core)
        for g in range(4):
            self.b.snd[a, g] = away[g * n:(g + 1) * n]

        @pl.when(t >= DEPTH.r0)
        def _():
            pl.semaphore_wait(self.s.c0, 1)
        self.core_copy(t, n).start()
        here = half_product(self.core)
        for g in range(4):
            self.b.own[o, g // 2, g % 2] = here[g * n:(g + 1) * n]

    def fill_small(self, small):
        k, n = SMALL_AT, SMALL_ROWS
        a, o = k % DEPTH.snd, k % DEPTH.own
        self.core_copy(k - DEPTH.snd, CHUNK_ROWS).wait_send()
        for g in range(4):
            self.b.snd[a, g, 0:n, :] = small[1 - self.core, g]
            self.b.own[o, g // 2, g % 2, 0:n, :] = small[self.core, g]
        pl.semaphore_wait(self.s.c0, 1)
        self.core_copy(k, n).start()

    def add_core(self, d, o, n):
        r = lax.rem(d, DEPTH.r0)
        self.core_copy(d, n).wait_recv()
        for g in range(4):
            self.b.own[o, g // 2, g % 2, 0:n] += self.b.r0[r, g, 0:n]

        @pl.when((d + DEPTH.r0 <= SMALL_AT) & (d + DEPTH.r0 != GAP))
        def _():
            pl.semaphore_signal(self.s.c0, inc=1, device_id=self.to_core, device_id_type=MESH_ID)

    def start_first(self, k, n, base):
        self.need(self.s.c1x, k, DEPTH.r1)
        self.need(self.s.c1y, k, DEPTH.r1)
        for copy in self.first_copies(k, n, base):
            copy.start()

    def stage_one(self, k, n):
        self.add_core(k, lax.rem(k, DEPTH.own), n)
        self.start_first(k, n, 0)

    def stage_pair(self, d):
        self.add_core(d, lax.rem(d + PERIOD, DEPTH.own), CHUNK_ROWS)

        @pl.when(d // PERIOD >= DEPTH.rp)
        def _():
            pl.semaphore_wait(self.s.cp, 1)
        self.pair_copy(d).start()

    def stage_one_pair(self, k):
        d = k - PERIOD
        o, r = lax.rem(k, DEPTH.own), lax.rem(d // PERIOD, DEPTH.rp)
        self.pair_copy(d).wait()
        rows = pl.ds(self.near, PAIR_ROWS)
        for g in range(4):
            self.b.own[o, g // 2, g % 2, rows] += self.b.rp[r, g // 2, g % 2]

        @pl.when(d + DEPTH.rp * PERIOD <= LAST_PAIR)
        def _():
            pl.semaphore_signal(self.s.cp, inc=1, device_id=self.to_pair, device_id_type=MESH_ID)
        self.start_first(k, PAIR_ROWS, self.near)

    def stage_two(self, k, n, base):
        o, r, half = lax.rem(k, DEPTH.own), lax.rem(k, DEPTH.r1), n // 2
        low, high = pl.ds(base, half), pl.ds(base + half, half)
        by_x, by_y = self.first_copies(k, n, base)
        by_x.wait_recv()
        for g in range(2):
            self.b.own[o, g, self.x, low, :] += self.b.r1x[r, g, 0:half]
        by_y.wait_recv()
        for g in range(2):
            self.b.own[o, self.y, g, high, :] += self.b.r1y[r, g, 0:half]
        self.grant(self.s.c1x, k, DEPTH.r1, self.to_x)
        self.grant(self.s.c1y, k, DEPTH.r1, self.to_y)
        by_x.wait_send()
        by_y.wait_send()
        self.need(self.s.c2x, k, DEPTH.r2)
        self.need(self.s.c2y, k, DEPTH.r2)
        for copy in self.second_copies(k, n, base):
            copy.start()

    def stage_three(self, k, n, base):
        o, r, half = lax.rem(k, DEPTH.own), lax.rem(k, DEPTH.r2), n // 2
        low, high = pl.ds(base, half), pl.ds(base + half, half)
        m = lax.rem(k, DEPTH.mid)
        by_x, by_y = self.second_copies(k, n, base)
        by_x.wait_recv()
        self.b.mid[m, high, :] = self.b.own[o, self.y, self.x, high, :] + self.b.r2x[r, 0:half]
        by_y.wait_recv()
        self.b.mid[m, low, :] = self.b.own[o, self.y, self.x, low, :] + self.b.r2y[r, 0:half]
        self.grant(self.s.c2x, k, DEPTH.r2, self.to_x)
        self.grant(self.s.c2y, k, DEPTH.r2, self.to_y)
        by_x.wait_send()
        by_y.wait_send()

        @pl.when(self.end)
        def _():
            self.need(self.s.c3, k, DEPTH.r3)
            self.inward_copy(k, n, base).start()

    def stage_four(self, k, n, paired):
        r = lax.rem(k, DEPTH.r3)
        part = PAIR_ROWS if paired else n

        @pl.when(self.end)
        def _():
            self.inward_copy(k, part, self.near if paired else 0).wait_send()

        @pl.when(self.inner)
        def _():
            self.inward_copy(k, part, 0).wait_recv()
            if paired:
                self.b.mid[lax.rem(k, DEPTH.mid), pl.ds(self.far, part), :] = self.b.r3[r, 0:part]
            else:
                self.mine(k, n)[...] += self.b.r3[r, 0:n]
            self.grant(self.s.c3, k, DEPTH.r3, self.to_pair)
            self.need(self.s.c4, k, DEPTH.r4)
            self.middle_copy(k, n).start()

    def stage_five(self, k, n):
        r = lax.rem(k, DEPTH.r4)

        @pl.when(self.inner)
        def _():
            self.middle_copy(k, n).wait()
            self.mine(k, n)[...] += self.b.r4[r, 0:n]
            self.grant(self.s.c4, k, DEPTH.r4, self.to_mid)
            self.outward_copy(k, n).start()
            self.keep_copy(k, n).start()

    def stage_six(self, k, n):
        @pl.when(self.inner)
        def _():
            self.outward_copy(k, n).wait_send()
        self.keep_copy(k, n).wait()

    def move(self, t):
        n = CHUNK_ROWS
        stages = (
            (LAG.one, lambda k: self.stage_one(k, n), self.stage_one_pair, lambda k: self.stage_one(k, SMALL_ROWS)),
            (LAG.two, lambda k: self.stage_two(k, n, 0), lambda k: self.stage_two(k, PAIR_ROWS, self.near),
             lambda k: self.stage_two(k, SMALL_ROWS, 0)),
            (LAG.three, lambda k: self.stage_three(k, n, 0), lambda k: self.stage_three(k, PAIR_ROWS, self.near),
             lambda k: self.stage_three(k, SMALL_ROWS, 0)),
            (LAG.four, lambda k: self.stage_four(k, n, False), lambda k: self.stage_four(k, n, True),
             lambda k: self.stage_four(k, SMALL_ROWS, False)),
            (LAG.five, lambda k: self.stage_five(k, n), None, lambda k: self.stage_five(k, SMALL_ROWS)),
            (LAG.six, lambda k: self.stage_six(k, n), None, lambda k: self.stage_six(k, SMALL_ROWS)),
        )
        behind = TAIL
        for lag, usual, paired, small in reversed(stages):
            k = t - behind
            odd = lax.rem(k + PERIOD, PERIOD) == 1
            if paired is None:
                pl.when((k >= 0) & (k < SMALL_AT) & (k != 1))(functools.partial(usual, k))
            else:
                pl.when((k >= 0) & (k < SMALL_AT) & jnp.logical_not(odd))(functools.partial(usual, k))
                pl.when(odd & (k > 1) & (k < SMALL_AT))(functools.partial(paired, k))
            pl.when(k == SMALL_AT)(functools.partial(small, k))
            behind -= lag
        d = t - LAG.one
        pl.when((lax.rem(d + PERIOD, PERIOD) == 1) & (d >= 0) & (d <= LAST_PAIR))(functools.partial(self.stage_pair, d))

    def step(self, t, half_product):
        self.move(t)
        self.fill(t, half_product)

    def finish(self, small):
        self.move(SMALL_AT)
        self.fill_small(small)

        def body(t, c):
            self.move(t)
            return c
        lax.fori_loop(SMALL_AT + 1, SMALL_AT + 1 + TAIL, body, 0)
        self.core_copy(GAP - DEPTH.snd, CHUNK_ROWS).wait_send()
        self.core_copy(GAP + 1, CHUNK_ROWS).wait_send()
        self.core_copy(SMALL_AT, SMALL_ROWS).wait_send()


def reducer_scratch():
    rows, cols, half, count, d = CHUNK_ROWS, CHUNK_COLS, CHUNK_ROWS // 2, SMALL_AT + 1, DEPTH
    vmem = lambda *shape: pltpu.VMEM(shape, jnp.float32)
    dma = lambda n: pltpu.SemaphoreType.DMA((n,))
    plain = pltpu.SemaphoreType.REGULAR
    bufs = Bunch(
        own=vmem(d.own, 2, 2, rows, cols), mid=vmem(d.mid, rows, cols), snd=vmem(d.snd, 4, rows, cols),
        r0=vmem(d.r0, 4, rows, cols), rp=vmem(d.rp, 2, 2, PAIR_ROWS, cols), r1x=vmem(d.r1, 2, half, cols),
        r1y=vmem(d.r1, 2, half, cols), r2x=vmem(d.r2, half, cols), r2y=vmem(d.r2, half, cols),
        r3=vmem(d.r3, rows, cols), r4=vmem(d.r4, rows, cols))
    sems = Bunch(
        snd=dma(d.snd), r0=dma(d.r0), sp=dma(d.rp), rp=dma(d.rp), out=dma(count), s1x=dma(d.r1), r1x=dma(d.r1),
        s1y=dma(d.r1), r1y=dma(d.r1), s2x=dma(d.r2), r2x=dma(d.r2), s2y=dma(d.r2), r2y=dma(d.r2), s3=dma(d.r3),
        r3=dma(d.r3), s4=dma(d.r4), r4=dma(d.r4), s5=dma(d.r4), c0=plain, cp=plain, c1x=plain, c1y=plain, c2x=plain,
        c2y=plain, c3=plain, c4=plain)
    return bufs, sems


class PartWriter:
    def __init__(self, bufs, sems, out_ref):
        self.b, self.s, self.out = bufs, sems, out_ref

    def enter(self):
        pass

    def step(self, t, half_product):
        for parity in range(2):
            value = half_product(parity)
            for g in range(4):
                self.b.own[parity, g // 2, g % 2] = value[g * 96:(g + 1) * 96]
        copy = pltpu.make_async_copy(self.b.own, self.out.at[t], self.s.out.at[0])
        copy.start()
        copy.wait()


def regroup(groups, refs):
    result, first = [], 0
    for names in groups:
        result.append(Bunch(**dict(zip(names, refs[first:first + len(names)]))))
        first += len(names)
    return result


def layer_kernel(groups, alone, *refs):
    given, hbm, out, vm, load, store, bufs, sems = regroup(groups, refs)
    reducer = (PartWriter if alone else Reducer)(bufs, sems, out.chunks)
    layer = Layer(given, hbm, out, vm, load, store)
    layer.reducer = reducer
    layer.forward(reducer.enter)
    layer.feed_forward()
    layer.backward_cross()
    layer.backward_self()

    if alone:
        def body(t, c):
            layer.advance(t)
            return c
        lax.fori_loop(24, CHUNKS, body, 0)
        entries = vm.memory_keys.shape[0]
        entry = lax.broadcasted_iota(jnp.int32, (4 * MEM_PAD, entries), 1)
        hit = jnp.where(layer.spread_ids(entries) == entry, 1.0, 0.0)
        out.mem_k[...] = tn(hit, vm.dmem_k[...], precision=lax.Precision.HIGHEST)
        out.mem_v[...] = tn(hit, vm.dmem_v[...], precision=lax.Precision.HIGHEST)
        out.gains[...] = vm.dgains[...]
        for h, row in enumerate(layer.bias_rows()):
            out.bias[h:h + 1, :] = row
    else:
        fill_small_rows(layer, vm)

        def body(t, c):
            left, value = layer.place(jnp.where(t > GAP, CHUNKS - 1, t))
            reducer.move(t)

            @pl.when(t != GAP)
            def _():
                reducer.fill(t, lambda parity: nn(vm.left[left, parity], value()))
            return c
        lax.fori_loop(24, SMALL_AT, body, 0)
        reducer.finish(vm.small)
    for copy in layer.stores():
        copy.wait()


def fill_small_rows(layer, vm):
    out_row = lax.broadcasted_iota(jnp.int32, (4 * MEM_PAD, 64), 1)
    entry = 4 * (out_row // 8) + lax.rem(out_row, 4)
    same = layer.spread_ids(64) == entry
    keys_row = lax.rem(out_row // 4, 2) == 0
    hit_k = jnp.where(same & keys_row, 1.0, 0.0)
    hit_v = jnp.where(same & jnp.logical_not(keys_row), 1.0, 0.0)
    memory = (tn(hit_k, vm.dmem_k[...], precision=lax.Precision.HIGHEST)
              + tn(hit_v, vm.dmem_v[...], precision=lax.Precision.HIGHEST))
    bias = jnp.concatenate(layer.bias_rows() + [jnp.zeros((4, LANES), F32)], axis=0)
    gains = jnp.concatenate([vm.dgains[...], jnp.zeros((5, 768), F32)], axis=0)
    for b in range(8):
        block = vm.small.at[b % 2, b // 2]
        for j in range(6):
            row, col = 8 * (j % 4), LANES * (j // 4)
            block[row:row + 8, col:col + LANES] = memory[8 * b:8 * b + 8, j * LANES:(j + 1) * LANES]
        turned = gains if b == 0 else pltpu.roll(gains, 768 - 96 * b, 1)
        block[16:24, LANES:2 * LANES] = turned[:, :LANES]
        block[24:32, LANES:2 * LANES] = jnp.zeros((8, LANES), F32)
        block[0:16, 2 * LANES:] = bias
        block[16:32, 2 * LANES:] = jnp.zeros((16, LANES), F32)


def call_grouped(kernel, ins, outs, scratch, **options):
    groups = [list(vars(g)) for g in ins + outs + scratch]
    pairs = lambda gs, i: [v[i] for g in gs for v in vars(g).values()]
    space = lambda gs: [pl.BlockSpec(memory_space=s) for s in pairs(gs, 1)]
    result = pl.pallas_call(
        functools.partial(kernel, groups), out_shape=pairs(outs, 0), in_specs=space(ins), out_specs=space(outs),
        scratch_shapes=[v for g in scratch for v in vars(g).values()], **options)(*pairs(ins, 0))
    return regroup(groups[len(ins):len(ins) + len(outs)], result)[0]


def in_space(space, **values):
    return Bunch(**{name: (value, space) for name, value in values.items()})


def run_layer(alone, hbm, given, tables):
    rows, width = hbm.tokens.shape
    enc_rows = hbm.encodings.shape[0]
    entries = hbm.memory_keys.shape[0]
    shape = jax.ShapeDtypeStruct
    outs = in_space(pl.ANY, layer_output=shape((rows, width), BF16), grad_tokens=shape((rows, width), BF16),
                    grad_encodings=shape((enc_rows, width), BF16))
    if alone:
        part = shape((entries, width), F32)
        vars(outs).update(vars(in_space(pl.ANY, chunks=shape((CHUNKS, 2, 2, 2, CHUNK_ROWS, CHUNK_COLS), F32))))
        vars(outs).update(vars(in_space(pltpu.VMEM, mem_k=part, mem_v=part, gains=shape((3, width), F32),
                                        bias=shape((12, LANES), F32))))
    else:
        vars(outs).update(vars(in_space(pl.ANY, chunks=shape((SMALL_AT + 1, CHUNK_ROWS, CHUNK_COLS), F32))))
    loaded = [name for name in vars(hbm) if vars(hbm)[name] is not hbm.ff_in and vars(hbm)[name] is not hbm.ff_out]
    vm = Bunch(**{name: pltpu.VMEM(vars(hbm)[name].shape, BF16) for name in loaded})
    big = lambda cols, kind: pltpu.VMEM((rows, cols), kind)
    vars(vm).update(
        wi=pltpu.VMEM((2, width, FF_TILE), BF16), wo=pltpu.VMEM((2, FF_TILE, width), BF16),
        hid=big(width, BF16), att=big(width, BF16), att2=big(width, BF16), right=big(RIGHT, BF16),
        left=pltpu.VMEM((10, 2, 384, rows), BF16),
        y1=big(width, F32), y2=big(width, F32), y3=big(width, F32), dh3=big(width, F32),
        z=big(FF_TILE, F32), dr=big(FF_TILE, F32), act=big(FF_TILE, BF16), dz=big(FF_TILE, BF16),
        bias=pltpu.VMEM((6, LANES, 2 * LANES), F32), dbias=pltpu.VMEM((6, LANES, 2 * LANES), F32),
        gains=pltpu.VMEM((3, width), F32), dgains=pltpu.VMEM((3, width), F32), up=pltpu.VMEM((LANES, width), BF16),
        mem_k=pltpu.VMEM((4, MEM_PAD, width), BF16), mem_v=pltpu.VMEM((4, MEM_PAD, width), BF16),
        dmem_k=pltpu.VMEM((4 * MEM_PAD, width), F32), dmem_v=pltpu.VMEM((4 * MEM_PAD, width), F32),
        layer_output=big(width, BF16), grad_tokens=big(width, BF16), grad_encodings=pltpu.VMEM((enc_rows, width), BF16),
        wi_sem=pltpu.SemaphoreType.DMA((2,)), wo_sem=pltpu.SemaphoreType.DMA((2,)))
    one = pltpu.SemaphoreType.DMA
    load = Bunch(**{name: one for name in loaded})
    store = Bunch(layer_output=one, grad_tokens=one, grad_encodings=one)
    bufs, sems = reducer_scratch()
    extra = dict(collective_id=0)
    if alone:
        bufs, sems = Bunch(own=pltpu.VMEM((2, 2, 2, CHUNK_ROWS, CHUNK_COLS), F32)), Bunch(out=pltpu.SemaphoreType.DMA((1,)))
        extra = {}
    else:
        vm.small = pltpu.VMEM((2, 4, SMALL_ROWS, CHUNK_COLS), F32)
    ins = [Bunch(**vars(in_space(pltpu.SMEM, lengths=given.lengths, ids=given.ids)),
                 **vars(in_space(pltpu.VMEM, gain_self=given.gain_self, gain_cross=given.gain_cross,
                                 gain_ff=given.gain_ff, rel_bias=given.rel_bias, tables=tables))),
           in_space(pl.ANY, **vars(hbm))]
    return call_grouped(
        lambda groups, *refs: layer_kernel(groups, alone, *refs), ins, [outs], [vm, load, store, bufs, sems],
        compiler_params=pltpu.CompilerParams(has_side_effects=True, vmem_limit_bytes=62 * 2**20, **extra),
        cost_estimate=pl.CostEstimate(flops=30 * 10**9, bytes_accessed=35 * 10**6, transcendentals=5 * 10**6))


FF_IN_AT, FF_OUT_AT, CROSS_OUT_AT, CROSS_Q_AT, CROSS_KV_AT, SELF_OUT_AT, SELF_QKV_AT = 0, 8, 16, 18, 20, 24, 26


def place_kernel(groups, *refs):
    given, tables, out, vm = regroup(groups, refs)
    slots = vm.sem
    chunk_in = lambda k: pltpu.make_async_copy(given.chunks.at[k], vm.chunks.at[k], slots.at[k])
    through = [(given.layer_output, vm.a, out.layer_output), (given.grad_tokens, vm.b, out.grad_tokens),
               (given.grad_encodings, vm.c, out.grad_encodings)]
    order = [SMALL_AT] + [number_of(d) for d in range(CHUNKS)]
    for k in order:
        chunk_in(k).start()
    for n, (src, mid, _) in enumerate(through):
        pltpu.make_async_copy(src, mid, slots.at[SMALL_AT + 1 + n]).start()
    made = []

    def send(src, dst):
        copy = pltpu.make_async_copy(src, dst, slots.at[SMALL_AT + 4 + len(made)])
        copy.start()
        made.append(copy)

    chunk_in(SMALL_AT).wait()
    small = vm.chunks[SMALL_AT, 0:SMALL_ROWS, :]
    for j in range(6):
        row, col = 8 * (j % 4), LANES * (j // 4)
        out.mem_k[:, j * LANES:(j + 1) * LANES] = small[row:row + 4, col:col + LANES]
        out.mem_v[:, j * LANES:(j + 1) * LANES] = small[row + 4:row + 8, col:col + LANES]
    for n, gain in enumerate((out.gain_self, out.gain_cross, out.gain_ff)):
        gain[...] = small[16 + n, LANES:LANES + 96]
    out.rel_bias[...] = nt(small[0:16, 2 * LANES:], tables.tables[1], precision=lax.Precision.HIGHEST)[0:12]
    pieces = ((out.ff_in, FF_IN_AT), (out.cross_out, CROSS_OUT_AT), (out.cross_q, CROSS_Q_AT),
              (out.cross_kv, CROSS_KV_AT), (out.self_out, SELF_OUT_AT), (out.self_qkv, SELF_QKV_AT))
    target = {}
    for ref, first in pieces:
        for k in range(ref.shape[1] // 384):
            target[first + k] = (ref, slice(0, 96), k * 384)
    for k in range(8):
        target[FF_OUT_AT + k] = (out.ff_out, slice((k // 2) * 96, (k // 2) * 96 + 96), (k % 2) * 384)
    for d in range(CHUNKS):
        k = number_of(d)
        chunk_in(k).wait()
        ref, at, col = target[d]
        send(vm.chunks.at[k], ref.at[at, col:col + CHUNK_COLS])
    for n, (src, mid, dst) in enumerate(through):
        pltpu.make_async_copy(src, mid, slots.at[SMALL_AT + 1 + n]).wait()
        send(mid, dst)
    for copy in made:
        copy.wait()


def place(done, tables):
    shape = jax.ShapeDtypeStruct
    outs = in_space(
        pl.ANY, layer_output=shape(done.layer_output.shape, BF16), grad_tokens=shape(done.grad_tokens.shape, BF16),
        grad_encodings=shape(done.grad_encodings.shape, BF16), ff_in=shape((96, 3072), F32), ff_out=shape((384, 768), F32),
        cross_out=shape((96, 768), F32), cross_q=shape((96, 768), F32), cross_kv=shape((96, 1536), F32),
        self_out=shape((96, 768), F32), self_qkv=shape((96, 2304), F32))
    gain = shape((96,), F32)
    vars(outs).update(vars(in_space(
        pltpu.VMEM, mem_k=shape((4, 768), F32), mem_v=shape((4, 768), F32), gain_self=gain, gain_cross=gain,
        gain_ff=gain, rel_bias=shape((12, 32), F32))))
    scratch = Bunch(
        chunks=pltpu.VMEM(done.chunks.shape, F32), a=pltpu.VMEM(done.layer_output.shape, BF16),
        b=pltpu.VMEM(done.grad_tokens.shape, BF16), c=pltpu.VMEM(done.grad_encodings.shape, BF16),
        sem=pltpu.SemaphoreType.DMA((SMALL_AT + 4 + CHUNKS + 3,)))
    return call_grouped(
        place_kernel, [in_space(pl.ANY, **vars(done)), in_space(pltpu.VMEM, tables=tables)], [outs], [scratch],
        compiler_params=pltpu.CompilerParams(vmem_limit_bytes=62 * 2**20),
        cost_estimate=pl.CostEstimate(flops=0, bytes_accessed=15 * 10**6, transcendentals=0))


def sum_alone(done, tables):
    chunks = done.chunks.transpose(0, 2, 3, 1, 4, 5).reshape(CHUNKS, 768, CHUNK_COLS)

    def whole(first, cols):
        part = chunks[first:first + cols // 384]
        return part.transpose(1, 0, 2).reshape(768, cols)

    ff_out = chunks[8:16].reshape(4, 2, 8, 96, CHUNK_COLS)
    parts = Bunch(
        ff_in=whole(FF_IN_AT, 3072), ff_out=ff_out.transpose(2, 0, 3, 1, 4).reshape(3072, 768),
        cross_out=whole(CROSS_OUT_AT, 768), cross_q=whole(CROSS_Q_AT, 768), cross_kv=whole(CROSS_KV_AT, 1536),
        self_out=whole(SELF_OUT_AT, 768), self_qkv=whole(SELF_QKV_AT, 2304), mem_k=done.mem_k, mem_v=done.mem_v,
        gain_self=done.gains[0], gain_cross=done.gains[1], gain_ff=done.gains[2])
    out = Bunch(**{name: lax.psum(lax.psum_scatter(value, "dp", scatter_dimension=0, tiled=True), "replica")
                   for name, value in vars(parts).items()})
    bias = lax.psum(done.bias, ("dp", "replica"))
    out.rel_bias = lax.dot_general(bias, tables[1], (((1,), (1,)), ((), ())), precision=lax.Precision.HIGHEST)
    out.layer_output, out.grad_tokens, out.grad_encodings = done.layer_output, done.grad_tokens, done.grad_encodings
    return out


def on_device(tokens, encodings, lengths, memory_ids, memory_keys, memory_values, gain_self, gain_cross, gain_ff,
              rel_bias, self_qkv, self_out, cross_q, cross_kv, cross_out, ff_in, ff_out, cotangent):
    width = tokens.shape[-1]
    alone = not (lax.axis_size("dp") == 8 and lax.axis_size("replica") == 4)
    hbm = Bunch(tokens=tokens.reshape(-1, width), encodings=encodings.reshape(-1, width),
                cotangent=cotangent.reshape(-1, width), memory_keys=memory_keys, memory_values=memory_values,
                self_qkv=self_qkv, self_out=self_out, cross_q=cross_q, cross_kv=cross_kv, cross_out=cross_out,
                ff_in=ff_in, ff_out=ff_out)
    given = Bunch(lengths=lengths, ids=memory_ids, gain_self=gain_self, gain_cross=gain_cross, gain_ff=gain_ff,
                  rel_bias=rel_bias.T)
    tables = jnp.asarray(bucket_tables(LANES, rel_bias.shape[0]))
    done = run_layer(alone, hbm, given, tables)
    out = sum_alone(done, tables) if alone else place(done, tables)
    return (
        out.layer_output.reshape(tokens.shape), out.grad_tokens.reshape(tokens.shape),
        out.grad_encodings.reshape(encodings.shape), out.gain_self, out.gain_cross, out.gain_ff, out.rel_bias.T,
        out.self_qkv, out.self_out, out.cross_q, out.cross_kv, out.cross_out, out.ff_in, out.ff_out, out.mem_k,
        out.mem_v)


def solution(mesh):
    split, whole = P(("dp", "replica")), P()
    return jax.shard_map(
        on_device,
        mesh=mesh,
        in_specs=(split,) * 4 + (whole,) * 13 + (split,),
        out_specs=(split,) * 3 + (P("dp"),) * 3 + (whole,) + (P("dp"),) * 9,
        check_vma=False,
    )
```

time: 904 us -> 208 us (0.23); the launches traced: 892 us -> 208 us
  waiting for transfers between devices: 494 us -> 0 us
  Pallas kernels: 0 us -> 207 us
  local copies, waits for them, and re-layouts: 171 us -> 0 us
  matrix products: 127 us -> 0 us
  blocking collectives: 61.9 us -> 0 us
  other arithmetic: 22.1 us -> 0 us
  between operations: 15.9 us -> 0.84 us
    reduce_scatter x6 -> x0, waiting for transfers between devices: 346 us -> none  [the longest x1 80.4 us: on_device(): lax.psum_scatter(d_ff_out, 'dp', scatter_dimension=0, tiled=True)]
    pallas_call x0 -> x2, Pallas kernels: none -> 207 us  [call_grouped(): pl.pallas_call(functools.partial(kernel, groups), out_shape=pairs(outs, 0...]
    psum x1 -> x0, waiting for transfers between devices: 148 us -> none  [on_device(): sum_self_qkv, sum_self_out = lax.psum((sf_a, sf_b), 'replica')]
    dot_general x34 -> x0, matrix products: 127 us -> none  [the longest x7 36.2 us: matmul_plain(): return jnp.dot(left, right, preferred_element_type=jnp.float32)]
    gather x6 -> x0, local copies, waits for them, and re-layouts: 74.9 us -> none  [the longest x2 67.4 us: on_device(): pos_bias = jnp.transpose(rel_bias[buckets], (2, 0, 1))]
    psum x2 -> x0, blocking collectives: 61.9 us -> none  [the longest x1 40.2 us: on_device(): lax.psum((d_rel_bias, d_gain_self, d_gain_cross, d_gain_ff), ('dp', 'repl...]
    unnamed x167 -> x0, local copies, waits for them, and re-layouts: 44.9 us -> none
    reshape x7 -> x0, local copies, waits for them, and re-layouts: 16.1 us -> none  [the longest x1 5.3 us: on_device(): qkv_all = matmul_plain(normed_one, self_qkv).astype(jnp.bfloat16).reshape...]
  transfers between devices with their start and end apart: 9 -> 0, of which waited for: 7 -> 0; matrix products, arithmetic and copies ran while one was open for 12% -> 0% of each run, Pallas kernels for 0% -> 0%
where the time goes in v1:
time: 208 us
  Pallas kernels  207 us (100%)
    pallas_call x2, Pallas kernels, call_grouped(): pl.pallas_call(functools.partial(kernel, groups), out_shape=pairs(outs, 0...  207 us

profile of v1, /device:TPU:0, one launch (start us, length us, event | category | flops | bytes accessed | tf_op | source)
XLA Modules:
  0.0 208.2 jit_solution(12372598502277618682)
XLA Ops:
  0.7 199.8 %shard_map.306 = (bf16[512,768]{1,0:T(8,128)(2,1)}, bf16[512,768]{1,0:T(8,128)(2,1)}, bf16[256,768]{1,0:T(8,128)(2,1)}, f32[34,96,384]{2,1,0:T(8,128)}) custom-call(s32[4]{0:T(128)} %refs_0_.1, s32[4,10]{1,0:T(4,128)} %refs_1_.1, f32[768]{0:T(1024)} %refs_2_.1, f32[768]{0:T(1024)} %refs_3_.1, f32[768]{0:T(1024)} %refs_4_.2, f32[12,32]{1,0:T(8,128)} %bitcast.14, ...), custom_call_target="tpu_custom_call" | custom-call | flops 30000001024 | bytes 35000000 | tf_op jit(solution)/shard_map/pallas_call | solution.py:854
  200.4 7.6 %shard_map.307 = (bf16[512,768]{1,0:T(8,128)(2,1)}, bf16[512,768]{1,0:T(8,128)(2,1)}, bf16[256,768]{1,0:T(8,128)(2,1)}, f32[96,3072]{1,0:T(8,128)}, f32[384,768]...) custom-call(bf16[512,768]{1,0:T(8,128)(2,1)} %get-tuple-element.36.r, ...), custom_call_target="tpu_custom_call" | custom-call | bytes 15000000 | tf_op jit(solution)/shard_map/pallas_call | solution.py:854

commit v2 on v1

--- a/solution.py
+++ b/solution.py
@@ -1,4 +1,5 @@
 import functools
+import itertools
 from types import SimpleNamespace as Bunch
 
 import jax
@@ -91,6 +92,7 @@
         vars(self).update(vars(given))
         vars(self).update(vars(vm))
         self.hbm, self.out, self.store = hbm, out, store
+        self.layer_output, self.grad_tokens = vm.cotangent, vm.att2
         self.questions, self.length, self.enc_len = 4, 128, 64
         self.rows = self.questions * self.length
         self.load = Bunch(**{name: pltpu.make_async_copy(vars(hbm)[name], vars(vm)[name], sem)
@@ -156,12 +158,8 @@
 
     def forward(self, enter):
         load = self.load
-        for copy in (load.tokens, load.self_qkv, load.encodings, load.cross_kv, load.memory_keys, load.memory_values,
-                     load.self_out, load.cross_q, load.cross_out):
+        for copy in (load.tokens, load.self_qkv, load.encodings, load.cross_kv):
             copy.start()
-        for copy in self.ff_loads(0) + self.ff_loads(1):
-            copy.start()
-        load.cotangent.start()
         enter()
         for n, gain in enumerate((self.gain_self, self.gain_cross, self.gain_ff)):
             self.gains[n:n + 1, :] = gain[...].reshape(1, gain.shape[0])
@@ -173,15 +171,32 @@
             at = self.q_rows(q)
             self.hid[at] = normed(self.tokens[at].astype(F32), self.gains[0:1])
             return c
-        lax.fori_loop(0, 4, norm_one, 0)
+        lax.fori_loop(0, 4, norm_one, 0, unroll=4)
         self.load.self_qkv.wait()
+        for copy in (load.memory_keys, load.memory_values, load.self_out, load.cross_q, load.cross_out, load.cotangent):
+            copy.start()
+        for copy in self.ff_loads(0) + self.ff_loads(1):
+            copy.start()
 
         def qkv_tile(j, c):
-            at = self.q_rows(j, 256)
-            right[:, pl.ds(pl.multiple_of(QKV + j * 256, 256), 256)] = nn(self.hid[...], self.self_qkv[:, at]).astype(BF16)
-            return c
-        lax.fori_loop(0, 9, qkv_tile, 0)
-
+            at = self.q_rows(j, 768)
+            right[:, pl.ds(pl.multiple_of(QKV + j * 768, 768), 768)] = nn(self.hid[...], self.self_qkv[:, at]).astype(BF16)
+            return c
+        lax.fori_loop(0, 3, qkv_tile, 0, unroll=3)
+
+        self.load.encodings.wait()
+        self.load.cross_kv.wait()
+        enc_rows = self.questions * self.enc_len
+
+        def ekv_tile(j, c):
+            at = self.q_rows(j, 768)
+            col = pl.ds(pl.multiple_of(EKV + j * 768, 768), 768)
+            right[0:enc_rows, col] = nn(self.encodings[...], self.cross_kv[:, at]).astype(BF16)
+            return c
+        lax.fori_loop(0, 2, ekv_tile, 0, unroll=2)
+        self.load.memory_keys.wait()
+        self.load.memory_values.wait()
+        self.memory_rows()
         m0, m1, _ = head_masks()
         allowed = self.causal()
 
@@ -193,41 +208,28 @@
                 probs = self.self_probs(q2, stacked(k2, m0, m1), p, allowed).astype(BF16)
                 self.att[at, lo:lo + LANES] = nn(probs, stacked(v2, m0, m1)).astype(BF16)
             return c
-        lax.fori_loop(0, 4, self_attention, 0)
-
-        self.load.encodings.wait()
-        self.load.cross_kv.wait()
-        enc_rows = self.questions * self.enc_len
-
-        def ekv_tile(j, c):
-            at = self.q_rows(j, 256)
-            col = pl.ds(pl.multiple_of(EKV + j * 256, 256), 256)
-            right[0:enc_rows, col] = nn(self.encodings[...], self.cross_kv[:, at]).astype(BF16)
-            return c
-        lax.fori_loop(0, 6, ekv_tile, 0)
-        self.load.memory_keys.wait()
-        self.load.memory_values.wait()
-        self.memory_rows()
+        lax.fori_loop(0, 4, self_attention, 0, unroll=4)
+
         self.load.self_out.wait()
 
         def out_tile(j, c):
-            at = self.q_rows(j, 256)
+            at = self.q_rows(j, 768)
             self.y1[:, at] = self.tokens[:, at].astype(F32) + nn(self.att[...], self.self_out[:, at])
             return c
-        lax.fori_loop(0, 3, out_tile, 0)
+        lax.fori_loop(0, 1, out_tile, 0, unroll=1)
 
         def norm_two(q, c):
             at = self.q_rows(q)
             self.hid[at] = normed(self.y1[at], self.gains[1:2])
             return c
-        lax.fori_loop(0, 4, norm_two, 0)
+        lax.fori_loop(0, 4, norm_two, 0, unroll=4)
         self.load.cross_q.wait()
 
         def cq_tile(j, c):
-            at = self.q_rows(j, 256)
-            right[:, pl.ds(pl.multiple_of(CQ + j * 256, 256), 256)] = nn(self.hid[...], self.cross_q[:, at]).astype(BF16)
-            return c
-        lax.fori_loop(0, 3, cq_tile, 0)
+            at = self.q_rows(j, 768)
+            right[:, pl.ds(pl.multiple_of(CQ + j * 768, 768), 768)] = nn(self.hid[...], self.cross_q[:, at]).astype(BF16)
+            return c
+        lax.fori_loop(0, 1, cq_tile, 0, unroll=1)
         present = self.present()
 
         def cross_attention(q, c):
@@ -239,14 +241,14 @@
                 probs = self.cross_probs(right[at, CQ + lo:CQ + lo + LANES], stacked(keys, m0, m1), present)
                 self.att2[at, lo:lo + LANES] = nn(probs.astype(BF16), stacked(vals, m0, m1)).astype(BF16)
             return c
-        lax.fori_loop(0, 4, cross_attention, 0)
+        lax.fori_loop(0, 4, cross_attention, 0, unroll=4)
         self.load.cross_out.wait()
 
         def out2_tile(j, c):
-            at = self.q_rows(j, 256)
+            at = self.q_rows(j, 768)
             self.y2[:, at] = self.y1[:, at] + nn(self.att2[...], self.cross_out[:, at])
             return c
-        lax.fori_loop(0, 3, out2_tile, 0)
+        lax.fori_loop(0, 1, out2_tile, 0, unroll=1)
         self.load.cotangent.wait()
 
         def norm_three(q, c):
@@ -258,7 +260,7 @@
             cot = jnp.where(valid, self.cotangent[at].astype(F32), 0.0)
             right[at, E3:E3 + 768] = cot.astype(BF16)
             return c
-        lax.fori_loop(0, 4, norm_three, 0)
+        lax.fori_loop(0, 4, norm_three, 0, unroll=4)
 
     def feed_forward(self):
         right = self.right
@@ -269,20 +271,14 @@
             slot = lax.rem(j, 2)
             for copy in self.ff_loads(j):
                 copy.wait()
-            self.z[...] = nn(self.hid[...], self.wi[slot])
-            self.dr[...] = nt(right[:, E3:E3 + 768], self.wo[slot])
-
-            def gelu(i, c):
-                at = pl.ds(pl.multiple_of(i * 32, 32), 32)
-                z = self.z[at]
+            for i in range(0, self.rows, 256):
+                at = slice(i, i + 256)
+                z = nn(self.hid[at], self.wi[slot])
+                dr = nt(right[at, E3:E3 + 768], self.wo[slot]).astype(BF16).astype(F32)
                 cdf = 0.5 * (1.0 + lax.erf(z * 0.7071067811865476))
                 pdf = jnp.exp(-0.5 * z * z) * 0.3989422804014327
                 self.act[at] = (z * cdf).astype(BF16)
-                dr = self.dr[at].astype(BF16).astype(F32)
                 self.dz[at] = (dr * (cdf + z * pdf)).astype(BF16)
-                return c
-            lax.fori_loop(0, 16, gelu, 0)
-
             act = self.act[...]
             dz = self.dz[...]
 
@@ -291,10 +287,8 @@
             for g in range(4):
                 at = pl.ds(pl.multiple_of((j // 2) * 96, 96), 96)
                 self.left[L_R + g, lax.rem(j, 2), at, :] = turned[g * 96:(g + 1) * 96]
-            for n in range(3):
-                at = slice(n * 256, (n + 1) * 256)
-                self.y3[:, at] += nn(act, self.wo[slot][:, at])
-                self.dh3[:, at] += nt(dz, self.wi[slot][at])
+            self.y3[...] += nn(act, self.wo[slot])
+            self.dh3[...] += nt(dz, self.wi[slot])
 
             @pl.when(j + 2 < 8)
             def _():
@@ -308,38 +302,56 @@
             valid = lax.broadcasted_iota(jnp.int32, (LANES, 1), 0) < self.lengths[q]
             self.layer_output[at] = jnp.where(valid, self.y3[at], 0.0).astype(BF16)
             return c
-        lax.fori_loop(0, 4, finish, 0)
+        lax.fori_loop(0, 4, finish, 0, unroll=4)
         self.stores()[0].start()
 
     def stores(self):
         return [pltpu.make_async_copy(vars(self)[name], vars(self.out)[name], sem) for name, sem in vars(self.store).items()]
+
+    def put_lefts(self, index, rows):
+        turned = rows.T
+        for b in range(8):
+            self.left[index, b % 2, (b // 2) * 96:(b // 2 + 1) * 96, 0:rows.shape[0]] = turned[b * 96:(b + 1) * 96]
+
+    def row_blocks(self):
+        return [slice(q * LANES, (q + 1) * LANES) for q in range(self.questions)]
+
+    def in_steps(self, first, parts):
+        count = sum(n for n, _ in parts)
+
+        def step(i, c):
+            at = 0
+            for n, part in parts:
+                pl.when((i >= at) & (i < at + n))(functools.partial(part, i - at))
+                at += n
+            self.advance(first + i)
+            return c
+        lax.fori_loop(0, count, step, 0)
 
     def backward_cross(self):
         right = self.right
         m0, m1, low_lanes = head_masks()
         present = self.present()
         enc_rows = self.questions * self.enc_len
-        self.dgains[...] = jnp.zeros_like(self.dgains)
-        self.left[L_ENC, :, :, enc_rows:] = jnp.zeros((2, 384, self.rows - enc_rows), BF16)
-        turned = self.encodings[...].T
-        for b in range(8):
-            self.left[L_ENC, b % 2, (b // 2) * 96:(b // 2 + 1) * 96, 0:enc_rows] = turned[b * 96:(b + 1) * 96]
-        right[enc_rows:, EKV:EKV + 1536] = jnp.zeros((self.rows - enc_rows, 1536), BF16)
 
         def pick(both):
             return jnp.where(low_lanes, both[:LANES], both[LANES:])
 
-        def question(q, c):
+        def before(_):
+            total = jnp.zeros((1, 768), F32)
+            for at in self.row_blocks():
+                back, gain = norm_pull(self.y2[at], self.gains[2:3], self.dh3[at])
+                total += gain
+                e2 = right[at, E3:E3 + 768].astype(F32) + back
+                self.y3[at] = e2
+                right[at, B2:B2 + 768] = e2.astype(BF16)
+            self.dgains[2:3] = total
+            self.up[...] = nt(right[:, B2:B2 + 768], self.cross_out[...]).astype(BF16)
+
+        def attention(q):
             at = self.q_rows(q)
             enc_at = self.q_rows(q, self.enc_len)
             mem_at = self.q_rows(q, MEM_PAD)
-            back, gain = norm_pull(self.y2[at], self.gains[2:3], self.dh3[at])
-            self.dgains[2:3] += gain
-            e2 = right[at, E3:E3 + 768].astype(F32) + back
-            self.y3[at] = e2
-            b2 = e2.astype(BF16)
-            right[at, B2:B2 + 768] = b2
-            self.up[...] = nt(b2, self.cross_out[...]).astype(BF16)
             for p in range(6):
                 lo = p * LANES
                 pair = slice(lo, lo + LANES)
@@ -347,7 +359,7 @@
                 vals = stacked(self.cross_side(q, p, self.mem_v, EKV + 768), m0, m1)
                 cq = right[at, CQ + lo:CQ + lo + LANES]
                 probs = self.cross_probs(cq, keys, present)
-                up = self.up[:, pair]
+                up = self.up[at, pair]
                 dvals = pick(tn(probs.astype(BF16), up))
                 ds = pair_pull(probs, nt(up, vals))
                 dkeys = pick(tn(ds, cq))
@@ -356,57 +368,77 @@
                 right[enc_at, EKV + 768 + lo:EKV + 768 + lo + LANES] = dvals[:64].astype(BF16)
                 self.dmem_k[mem_at, pair] = dkeys[64:64 + MEM_PAD]
                 self.dmem_v[mem_at, pair] = dvals[64:64 + MEM_PAD]
-                if p == 2:
-                    self.advance(8 + 2 * q)
-            self.grad_encodings[enc_at] = nt(right[enc_at, EKV:EKV + 1536], self.cross_kv[...]).astype(BF16)
-            y1 = self.y1[at]
-            back, gain = norm_pull(y1, self.gains[1:2], nt(right[at, CQ:CQ + 768], self.cross_q[...]))
-            self.dgains[1:2] += gain
-            self.y3[at] += back
-            self.put_left(L_H2, q, normed(y1, self.gains[1:2]))
-            self.put_left(L_O2, q, self.att2[at])
-            self.advance(9 + 2 * q)
-            return c
-        lax.fori_loop(0, 4, question, 0)
+
+        def after(_):
+            self.dh3[...] = nt(right[:, CQ:CQ + 768], self.cross_q[...])
+            total = jnp.zeros((1, 768), F32)
+            for at in self.row_blocks():
+                back, gain = norm_pull(self.y1[at], self.gains[1:2], self.dh3[at])
+                total += gain
+                self.y3[at] += back
+            self.dgains[1:2] = total
+
+        def turn(_):
+            for at in self.row_blocks():
+                self.hid[at] = normed(self.y1[at], self.gains[1:2])
+            self.put_lefts(L_H2, self.hid[...])
+            self.put_lefts(L_O2, self.att2[...])
+
+        def encodings(_):
+            self.put_lefts(L_ENC, self.encodings[...])
+            self.left[L_ENC, :, :, enc_rows:] = jnp.zeros((2, 384, self.rows - enc_rows), BF16)
+            right[enc_rows:, EKV:EKV + 1536] = jnp.zeros((self.rows - enc_rows, 1536), BF16)
+            self.grad_encodings[...] = nt(right[0:enc_rows, EKV:EKV + 1536], self.cross_kv[...]).astype(BF16)
+
+        self.in_steps(8, ((1, before), (4, attention), (1, after), (1, turn), (1, encodings)))
 
     def backward_self(self):
         right = self.right
         m0, m1, low_lanes = head_masks()
         allowed = self.causal()
-        self.dbias[...] = jnp.zeros_like(self.dbias)
 
         def pick(both):
             return jnp.where(low_lanes, both[:LANES], both[LANES:])
 
-        def question(q, c):
+        def before(_):
+            self.dbias[...] = jnp.zeros_like(self.dbias)
+            right[:, B1:B1 + 768] = self.y3[...].astype(BF16)
+            self.up[...] = nt(right[:, B1:B1 + 768], self.self_out[...]).astype(BF16)
+
+        def attention(q):
             at = self.q_rows(q)
-            b1 = self.y3[at].astype(BF16)
-            right[at, B1:B1 + 768] = b1
-            self.up[...] = nt(b1, self.self_out[...]).astype(BF16)
             for p in range(6):
                 lo = p * LANES
-                pair = slice(lo, lo + LANES)
                 q2, k2, v2 = (right[at, QKV + 768 * i + lo:QKV + 768 * i + lo + LANES] for i in range(3))
                 keys = stacked(k2, m0, m1)
                 probs = self.self_probs(q2, keys, p, allowed)
-                up = self.up[:, pair]
+                up = self.up[at, lo:lo + LANES]
                 dval = pick(tn(probs.astype(BF16), up))
                 ds = pair_pull(probs, nt(up, stacked(v2, m0, m1)))
                 self.dbias[p] += ds.astype(F32)
                 right[at, QKV + lo:QKV + lo + LANES] = nn(ds, keys).astype(BF16)
                 right[at, QKV + 768 + lo:QKV + 768 + lo + LANES] = pick(tn(ds, q2)).astype(BF16)
                 right[at, QKV + 1536 + lo:QKV + 1536 + lo + LANES] = dval.astype(BF16)
-                if p == 2:
-                    self.advance(16 + 2 * q)
-            tok = self.tokens[at].astype(F32)
-            back, gain = norm_pull(tok, self.gains[0:1], nt(right[at, QKV:QKV + 2304], self.self_qkv[...]))
-            self.dgains[0:1] += gain
-            self.grad_tokens[at] = (self.y3[at] + back).astype(BF16)
-            self.put_left(L_H1, q, normed(tok, self.gains[0:1]))
-            self.put_left(L_O, q, self.att[at])
-            self.advance(17 + 2 * q)
-            return c
-        lax.fori_loop(0, 4, question, 0)
+
+        def after(_):
+            self.dh3[...] = nt(right[:, QKV:QKV + 2304], self.self_qkv[...])
+
+        def finish(_):
+            total = jnp.zeros((1, 768), F32)
+            for at in self.row_blocks():
+                tok = self.tokens[at].astype(F32)
+                back, gain = norm_pull(tok, self.gains[0:1], self.dh3[at])
+                total += gain
+                self.grad_tokens[at] = (self.y3[at] + back).astype(BF16)
+            self.dgains[0:1] = total
+
+        def turn(_):
+            for at in self.row_blocks():
+                self.hid[at] = normed(self.tokens[at].astype(F32), self.gains[0:1])
+            self.put_lefts(L_H1, self.hid[...])
+            self.put_lefts(L_O, self.att[...])
+
+        self.in_steps(16, ((1, before), (4, attention), (1, after), (1, finish), (1, turn)))
         for copy in self.stores()[1:]:
             copy.start()
 
@@ -448,18 +480,21 @@
 
 
 MESH_ID = pl.DeviceIdType.MESH
-CHUNK_ROWS, CHUNK_COLS, PAIR_ROWS, SMALL_ROWS = 96, 384, 48, 32
-PERIOD, GAP, LAST_PAIR, SMALL_AT = 5, 31, 26, 33
-CHUNKS = 32
-DEPTH = Bunch(own=12, mid=8, snd=3, r0=3, rp=2, r1=4, r2=4, r3=4, r4=4)
-LAG = Bunch(one=1, two=2, three=2, four=2, five=2, six=2)
-TAIL = sum(vars(LAG).values())
-
-
-def number_of(d):
-    if d == CHUNKS - 1:
-        return GAP + 1
-    return d + PERIOD if d % PERIOD == 1 else d
+CHUNK_ROWS, CHUNK_COLS, PAIR_ROWS, SMALL_ROWS = 96, 384, 48, 48
+PERIOD, GAP, LAST_PAIR, SMALL_FROM, LAST = 5, 26, 21, 29, 37
+CHUNKS, SPLIT = 32, 4
+DEPTH = Bunch(own=12, mid=10, snd=3, r0=3, rp=2, r1=6, r2=5, r3=5, r4=5)
+LAG = Bunch(one=1, two=3, three=2, four=2, five=2, six=3)
+LATE = Bunch(one=1, two=3, three=2, four=2, five=3, six=3)
+
+
+def after(lags):
+    return list(itertools.accumulate(vars(lags).values()))
+
+
+def data_of(k):
+    pair = (lax.rem(k, PERIOD) == 1) & (k <= GAP)
+    return jnp.where(pair, k - PERIOD, jnp.where(k > GAP, k - 1, k))
 
 
 class Reducer:
@@ -534,15 +569,24 @@
         r = lax.rem(k, DEPTH.r4)
         return self.copy(self.mine(k, n), self.b.r4.at[r, pl.ds(0, n)], self.s.s4.at[r], self.s.r4.at[r], self.to_mid)
 
+    def result(self, k, n):
+        if n == SMALL_ROWS:
+            last = k == LAST
+            u = k - SMALL_FROM
+            row, d = jnp.where(last, 0, lax.rem(u, 2) * SMALL_ROWS), jnp.where(last, CHUNKS, CHUNKS - SPLIT + u // 2)
+        else:
+            row, d = 0, data_of(k)
+        return self.out.at[pl.ds(pl.multiple_of(row, 8), n), pl.ds(pl.multiple_of(d * CHUNK_COLS, LANES), CHUNK_COLS)]
+
     def outward_copy(self, k, n):
         r = lax.rem(k, DEPTH.r4)
-        return self.copy(self.mine(k, n), self.out.at[k, pl.ds(0, n)], self.s.s5.at[r], self.s.out.at[k], self.to_pair)
+        return self.copy(self.mine(k, n), self.result(k, n), self.s.s5.at[r], self.s.out.at[k], self.to_pair)
 
     def keep_copy(self, k, n):
-        return pltpu.make_async_copy(self.mine(k, n), self.out.at[k, pl.ds(0, n)], self.s.out.at[k])
+        return pltpu.make_async_copy(self.mine(k, n), self.result(k, n), self.s.out.at[k])
 
     def grant(self, sem, k, depth, target):
-        @pl.when(k + depth <= SMALL_AT)
+        @pl.when(k + depth <= LAST)
         def _():
             pl.semaphore_signal(sem, inc=1, device_id=target, device_id_type=MESH_ID)
 
@@ -550,6 +594,9 @@
         @pl.when((k >= depth) & (k != depth + 1))
         def _():
             pl.semaphore_wait(sem, 1)
+
+    def before(self, t):
+        return t - jnp.where(t == GAP + DEPTH.snd, 2 * DEPTH.snd, DEPTH.snd)
 
     def fill(self, t, half_product):
         n = CHUNK_ROWS
@@ -558,13 +605,13 @@
 
         @pl.when(t >= DEPTH.snd)
         def _():
-            self.core_copy(t - DEPTH.snd, n).wait_send()
+            self.core_copy(self.before(t), n).wait_send()
 
         away = half_product(1 - self.core)
         for g in range(4):
             self.b.snd[a, g] = away[g * n:(g + 1) * n]
 
-        @pl.when(t >= DEPTH.r0)
+        @pl.when((t >= DEPTH.r0) & (t != GAP + DEPTH.r0))
         def _():
             pl.semaphore_wait(self.s.c0, 1)
         self.core_copy(t, n).start()
@@ -572,15 +619,26 @@
         for g in range(4):
             self.b.own[o, g // 2, g % 2] = here[g * n:(g + 1) * n]
 
-    def fill_small(self, small):
-        k, n = SMALL_AT, SMALL_ROWS
-        a, o = k % DEPTH.snd, k % DEPTH.own
-        self.core_copy(k - DEPTH.snd, CHUNK_ROWS).wait_send()
+    def fill_small(self, k, part):
+        n = SMALL_ROWS
+        a, o = lax.rem(k, DEPTH.snd), lax.rem(k, DEPTH.own)
+
+        @pl.when(k - DEPTH.snd < SMALL_FROM)
+        def _():
+            self.core_copy(self.before(k), CHUNK_ROWS).wait_send()
+
+        @pl.when(k - DEPTH.snd >= SMALL_FROM)
+        def _():
+            self.core_copy(k - DEPTH.snd, n).wait_send()
+        self.b.snd[a, :, 0:n, :] = part(1 - self.core)
+
+        @pl.when(k != GAP + DEPTH.r0)
+        def _():
+            pl.semaphore_wait(self.s.c0, 1)
+        self.core_copy(k, n).start()
+        here = part(self.core)
         for g in range(4):
-            self.b.snd[a, g, 0:n, :] = small[1 - self.core, g]
-            self.b.own[o, g // 2, g % 2, 0:n, :] = small[self.core, g]
-        pl.semaphore_wait(self.s.c0, 1)
-        self.core_copy(k, n).start()
+            self.b.own[o, g // 2, g % 2, 0:n, :] = here[g]
 
     def add_core(self, d, o, n):
         r = lax.rem(d, DEPTH.r0)
@@ -588,7 +646,7 @@
         for g in range(4):
             self.b.own[o, g // 2, g % 2, 0:n] += self.b.r0[r, g, 0:n]
 
-        @pl.when((d + DEPTH.r0 <= SMALL_AT) & (d + DEPTH.r0 != GAP))
+        @pl.when((d + DEPTH.r0 <= LAST) & (d + DEPTH.r0 != GAP))
         def _():
             pl.semaphore_signal(self.s.c0, inc=1, device_id=self.to_core, device_id_type=MESH_ID)
 
@@ -697,52 +755,62 @@
             self.outward_copy(k, n).wait_send()
         self.keep_copy(k, n).wait()
 
+    def stages(self):
+        n, small, pair = CHUNK_ROWS, SMALL_ROWS, PAIR_ROWS
+        return (
+            (lambda k: self.stage_one(k, n), self.stage_one_pair, lambda k: self.stage_one(k, small)),
+            (lambda k: self.stage_two(k, n, 0), lambda k: self.stage_two(k, pair, self.near),
+             lambda k: self.stage_two(k, small, 0)),
+            (lambda k: self.stage_three(k, n, 0), lambda k: self.stage_three(k, pair, self.near),
+             lambda k: self.stage_three(k, small, 0)),
+            (lambda k: self.stage_four(k, n, False), lambda k: self.stage_four(k, n, True),
+             lambda k: self.stage_four(k, small, False)),
+            (lambda k: self.stage_five(k, n), None, lambda k: self.stage_five(k, small)),
+            (lambda k: self.stage_six(k, n), None, lambda k: self.stage_six(k, small)),
+        )
+
     def move(self, t):
-        n = CHUNK_ROWS
-        stages = (
-            (LAG.one, lambda k: self.stage_one(k, n), self.stage_one_pair, lambda k: self.stage_one(k, SMALL_ROWS)),
-            (LAG.two, lambda k: self.stage_two(k, n, 0), lambda k: self.stage_two(k, PAIR_ROWS, self.near),
-             lambda k: self.stage_two(k, SMALL_ROWS, 0)),
-            (LAG.three, lambda k: self.stage_three(k, n, 0), lambda k: self.stage_three(k, PAIR_ROWS, self.near),
-             lambda k: self.stage_three(k, SMALL_ROWS, 0)),
-            (LAG.four, lambda k: self.stage_four(k, n, False), lambda k: self.stage_four(k, n, True),
-             lambda k: self.stage_four(k, SMALL_ROWS, False)),
-            (LAG.five, lambda k: self.stage_five(k, n), None, lambda k: self.stage_five(k, SMALL_ROWS)),
-            (LAG.six, lambda k: self.stage_six(k, n), None, lambda k: self.stage_six(k, SMALL_ROWS)),
-        )
-        behind = TAIL
-        for lag, usual, paired, small in reversed(stages):
+        for behind, (usual, paired, small) in reversed(list(zip(after(LAG), self.stages()))):
             k = t - behind
-            odd = lax.rem(k + PERIOD, PERIOD) == 1
+            odd = (lax.rem(k + PERIOD, PERIOD) == 1) & (k <= GAP)
             if paired is None:
-                pl.when((k >= 0) & (k < SMALL_AT) & (k != 1))(functools.partial(usual, k))
+                pl.when((k >= 0) & (k < SMALL_FROM) & (k != 1))(functools.partial(usual, k))
             else:
-                pl.when((k >= 0) & (k < SMALL_AT) & jnp.logical_not(odd))(functools.partial(usual, k))
-                pl.when(odd & (k > 1) & (k < SMALL_AT))(functools.partial(paired, k))
-            pl.when(k == SMALL_AT)(functools.partial(small, k))
-            behind -= lag
+                pl.when((k >= 0) & (k < SMALL_FROM) & jnp.logical_not(odd))(functools.partial(usual, k))
+                pl.when(odd & (k > 1))(functools.partial(paired, k))
+            pl.when((k >= SMALL_FROM) & (k <= LAST))(functools.partial(small, k))
         d = t - LAG.one
         pl.when((lax.rem(d + PERIOD, PERIOD) == 1) & (d >= 0) & (d <= LAST_PAIR))(functools.partial(self.stage_pair, d))
+
+    def drain(self):
+        left = []
+        for number, (due, order) in enumerate(zip(after(LAG), after(LATE))):
+            left += [(k + order, -number, k) for k in range(LAST + 1) if k + due > LAST]
+        for _, number, k in sorted(left):
+            usual, paired, small = self.stages()[-number]
+            odd = k % PERIOD == 1 and k <= GAP
+            (small if k >= SMALL_FROM else paired if odd and paired is not None else usual)(jnp.int32(k))
 
     def step(self, t, half_product):
         self.move(t)
         self.fill(t, half_product)
 
-    def finish(self, small):
-        self.move(SMALL_AT)
-        self.fill_small(small)
-
-        def body(t, c):
-            self.move(t)
-            return c
-        lax.fori_loop(SMALL_AT + 1, SMALL_AT + 1 + TAIL, body, 0)
-        self.core_copy(GAP - DEPTH.snd, CHUNK_ROWS).wait_send()
-        self.core_copy(GAP + 1, CHUNK_ROWS).wait_send()
-        self.core_copy(SMALL_AT, SMALL_ROWS).wait_send()
+    def finish(self, half, small):
+        def body(k, c):
+            self.move(k)
+            self.fill_small(k, lambda parity: half(parity, k - SMALL_FROM))
+            return c
+        lax.fori_loop(SMALL_FROM, LAST, body, 0)
+        self.move(LAST)
+        self.fill_small(LAST, lambda parity: small[parity])
+
+        self.drain()
+        for back in range(DEPTH.snd):
+            self.core_copy(LAST - back, SMALL_ROWS).wait_send()
 
 
 def reducer_scratch():
-    rows, cols, half, count, d = CHUNK_ROWS, CHUNK_COLS, CHUNK_ROWS // 2, SMALL_AT + 1, DEPTH
+    rows, cols, half, count, d = CHUNK_ROWS, CHUNK_COLS, CHUNK_ROWS // 2, LAST + 1, DEPTH
     vmem = lambda *shape: pltpu.VMEM(shape, jnp.float32)
     dma = lambda n: pltpu.SemaphoreType.DMA((n,))
     plain = pltpu.SemaphoreType.REGULAR
@@ -811,15 +879,21 @@
         fill_small_rows(layer, vm)
 
         def body(t, c):
-            left, value = layer.place(jnp.where(t > GAP, CHUNKS - 1, t))
+            left, value = layer.place(jnp.where(t > GAP, t - 1, t))
             reducer.move(t)
 
             @pl.when(t != GAP)
             def _():
                 reducer.fill(t, lambda parity: nn(vm.left[left, parity], value()))
             return c
-        lax.fori_loop(24, SMALL_AT, body, 0)
-        reducer.finish(vm.small)
+        lax.fori_loop(24, SMALL_FROM, body, 0)
+
+        def half(parity, u):
+            left, value = layer.place(CHUNKS - SPLIT + u // 2)
+            at = lambda g: pl.ds(pl.multiple_of(g * 96 + lax.rem(u, 2) * SMALL_ROWS, SMALL_ROWS), SMALL_ROWS)
+            rows = jnp.concatenate([vm.left[left, parity, at(g)] for g in range(4)], axis=0)
+            return nn(rows, value()).reshape(4, SMALL_ROWS, CHUNK_COLS)
+        reducer.finish(half, vm.small)
     for copy in layer.stores():
         copy.wait()
 
@@ -845,6 +919,7 @@
         block[24:32, LANES:2 * LANES] = jnp.zeros((8, LANES), F32)
         block[0:16, 2 * LANES:] = bias
         block[16:32, 2 * LANES:] = jnp.zeros((16, LANES), F32)
+        block[32:, :] = jnp.zeros((SMALL_ROWS - 32, CHUNK_COLS), F32)
 
 
 def call_grouped(kernel, ins, outs, scratch, **options):
@@ -874,7 +949,7 @@
         vars(outs).update(vars(in_space(pltpu.VMEM, mem_k=part, mem_v=part, gains=shape((3, width), F32),
                                         bias=shape((12, LANES), F32))))
     else:
-        vars(outs).update(vars(in_space(pl.ANY, chunks=shape((SMALL_AT + 1, CHUNK_ROWS, CHUNK_COLS), F32))))
+        vars(outs).update(vars(in_space(pl.ANY, chunks=shape((CHUNK_ROWS, (CHUNKS + 1) * CHUNK_COLS), F32))))
     loaded = [name for name in vars(hbm) if vars(hbm)[name] is not hbm.ff_in and vars(hbm)[name] is not hbm.ff_out]
     vm = Bunch(**{name: pltpu.VMEM(vars(hbm)[name].shape, BF16) for name in loaded})
     big = lambda cols, kind: pltpu.VMEM((rows, cols), kind)
@@ -883,12 +958,12 @@
         hid=big(width, BF16), att=big(width, BF16), att2=big(width, BF16), right=big(RIGHT, BF16),
         left=pltpu.VMEM((10, 2, 384, rows), BF16),
         y1=big(width, F32), y2=big(width, F32), y3=big(width, F32), dh3=big(width, F32),
-        z=big(FF_TILE, F32), dr=big(FF_TILE, F32), act=big(FF_TILE, BF16), dz=big(FF_TILE, BF16),
+        act=big(FF_TILE, BF16), dz=big(FF_TILE, BF16),
         bias=pltpu.VMEM((6, LANES, 2 * LANES), F32), dbias=pltpu.VMEM((6, LANES, 2 * LANES), F32),
-        gains=pltpu.VMEM((3, width), F32), dgains=pltpu.VMEM((3, width), F32), up=pltpu.VMEM((LANES, width), BF16),
+        gains=pltpu.VMEM((3, width), F32), dgains=pltpu.VMEM((3, width), F32), up=big(width, BF16),
         mem_k=pltpu.VMEM((4, MEM_PAD, width), BF16), mem_v=pltpu.VMEM((4, MEM_PAD, width), BF16),
         dmem_k=pltpu.VMEM((4 * MEM_PAD, width), F32), dmem_v=pltpu.VMEM((4 * MEM_PAD, width), F32),
-        layer_output=big(width, BF16), grad_tokens=big(width, BF16), grad_encodings=pltpu.VMEM((enc_rows, width), BF16),
+        grad_encodings=pltpu.VMEM((enc_rows, width), BF16),
         wi_sem=pltpu.SemaphoreType.DMA((2,)), wo_sem=pltpu.SemaphoreType.DMA((2,)))
     one = pltpu.SemaphoreType.DMA
     load = Bunch(**{name: one for name in loaded})
@@ -915,49 +990,44 @@
 
 def place_kernel(groups, *refs):
     given, tables, out, vm = regroup(groups, refs)
-    slots = vm.sem
-    chunk_in = lambda k: pltpu.make_async_copy(given.chunks.at[k], vm.chunks.at[k], slots.at[k])
-    through = [(given.layer_output, vm.a, out.layer_output), (given.grad_tokens, vm.b, out.grad_tokens),
-               (given.grad_encodings, vm.c, out.grad_encodings)]
-    order = [SMALL_AT] + [number_of(d) for d in range(CHUNKS)]
-    for k in order:
-        chunk_in(k).start()
-    for n, (src, mid, _) in enumerate(through):
-        pltpu.make_async_copy(src, mid, slots.at[SMALL_AT + 1 + n]).start()
-    made = []
-
-    def send(src, dst):
-        copy = pltpu.make_async_copy(src, dst, slots.at[SMALL_AT + 4 + len(made)])
-        copy.start()
-        made.append(copy)
-
-    chunk_in(SMALL_AT).wait()
-    small = vm.chunks[SMALL_AT, 0:SMALL_ROWS, :]
+    sems = iter(range(vm.sem.shape[0]))
+    copy = lambda src, dst: pltpu.make_async_copy(src, dst, vm.sem.at[next(sems)])
+    small_at = slice(CHUNKS * CHUNK_COLS, (CHUNKS + 1) * CHUNK_COLS)
+    small = copy(given.chunks.at[0:SMALL_ROWS, small_at], vm.chunks.at[0:SMALL_ROWS, small_at])
+    small.start()
+    pieces = ((out.ff_in, FF_IN_AT), (out.ff_out, FF_OUT_AT), (out.cross_out, CROSS_OUT_AT), (out.cross_q, CROSS_Q_AT),
+              (out.cross_kv, CROSS_KV_AT), (out.self_out, SELF_OUT_AT), (out.self_qkv, SELF_QKV_AT))
+    moves = []
+    for ref, first in pieces:
+        cols = ref.shape[0] * ref.shape[1] // CHUNK_ROWS
+        at = slice(first * CHUNK_COLS, first * CHUNK_COLS + cols)
+        targets = [(vm.chunks.at[:, at], ref)]
+        if first == FF_OUT_AT:
+            targets = [(vm.chunks.at[:, (first + k) * CHUNK_COLS:(first + k + 1) * CHUNK_COLS],
+                        ref.at[(k // 2) * 96:(k // 2) * 96 + 96, (k % 2) * CHUNK_COLS:(k % 2 + 1) * CHUNK_COLS])
+                       for k in range(8)]
+        moves.append((copy(given.chunks.at[:, at], vm.chunks.at[:, at]), [copy(*pair) for pair in targets]))
+    for src, mid, dst in ((given.layer_output, vm.a, out.layer_output), (given.grad_tokens, vm.b, out.grad_tokens),
+                          (given.grad_encodings, vm.c, out.grad_encodings)):
+        moves.append((copy(src, mid), [copy(mid, dst)]))
+    for into, _ in moves:
+        into.start()
+    small.wait()
+    sums = vm.chunks[0:SMALL_ROWS, small_at]
     for j in range(6):
         row, col = 8 * (j % 4), LANES * (j // 4)
-        out.mem_k[:, j * LANES:(j + 1) * LANES] = small[row:row + 4, col:col + LANES]
-        out.mem_v[:, j * LANES:(j + 1) * LANES] = small[row + 4:row + 8, col:col + LANES]
+        out.mem_k[:, j * LANES:(j + 1) * LANES] = sums[row:row + 4, col:col + LANES]
+        out.mem_v[:, j * LANES:(j + 1) * LANES] = sums[row + 4:row + 8, col:col + LANES]
     for n, gain in enumerate((out.gain_self, out.gain_cross, out.gain_ff)):
-        gain[...] = small[16 + n, LANES:LANES + 96]
-    out.rel_bias[...] = nt(small[0:16, 2 * LANES:], tables.tables[1], precision=lax.Precision.HIGHEST)[0:12]
-    pieces = ((out.ff_in, FF_IN_AT), (out.cross_out, CROSS_OUT_AT), (out.cross_q, CROSS_Q_AT),
-              (out.cross_kv, CROSS_KV_AT), (out.self_out, SELF_OUT_AT), (out.self_qkv, SELF_QKV_AT))
-    target = {}
-    for ref, first in pieces:
-        for k in range(ref.shape[1] // 384):
-            target[first + k] = (ref, slice(0, 96), k * 384)
-    for k in range(8):
-        target[FF_OUT_AT + k] = (out.ff_out, slice((k // 2) * 96, (k // 2) * 96 + 96), (k % 2) * 384)
-    for d in range(CHUNKS):
-        k = number_of(d)
-        chunk_in(k).wait()
-        ref, at, col = target[d]
-        send(vm.chunks.at[k], ref.at[at, col:col + CHUNK_COLS])
-    for n, (src, mid, dst) in enumerate(through):
-        pltpu.make_async_copy(src, mid, slots.at[SMALL_AT + 1 + n]).wait()
-        send(mid, dst)
-    for copy in made:
-        copy.wait()
+        gain[...] = sums[16 + n, LANES:LANES + 96]
+    out.rel_bias[...] = nt(sums[0:16, 2 * LANES:], tables.tables[1], precision=lax.Precision.HIGHEST)[0:12]
+    for into, onward in moves:
+        into.wait()
+        for move in onward:
+            move.start()
+    for _, onward in moves:
+        for move in onward:
+            move.wait()
 
 
 def place(done, tables):
@@ -974,7 +1044,7 @@
     scratch = Bunch(
         chunks=pltpu.VMEM(done.chunks.shape, F32), a=pltpu.VMEM(done.layer_output.shape, BF16),
         b=pltpu.VMEM(done.grad_tokens.shape, BF16), c=pltpu.VMEM(done.grad_encodings.shape, BF16),
-        sem=pltpu.SemaphoreType.DMA((SMALL_AT + 4 + CHUNKS + 3,)))
+        sem=pltpu.SemaphoreType.DMA((28,)))
     return call_grouped(
         place_kernel, [in_space(pl.ANY, **vars(done)), in_space(pltpu.VMEM, tables=tables)], [outs], [scratch],
         compiler_params=pltpu.CompilerParams(vmem_limit_bytes=62 * 2**20),

time: 208 us -> 191 us (0.918)
  Pallas kernels: 207 us -> 190 us
    pallas_call x2, Pallas kernels: 207 us -> 190 us  [call_grouped(): pl.pallas_call(functools.partial(kernel, groups), out_shape=pairs(outs, 0...]
where the time goes in v2:
time: 191 us
  Pallas kernels  190 us (99%)
    pallas_call x2, Pallas kernels, call_grouped(): pl.pallas_call(functools.partial(kernel, groups), out_shape=pairs(outs, 0...  190 us

profile of v2, /device:TPU:0, one launch (start us, length us, event | category | flops | bytes accessed | tf_op | source)
XLA Modules:
  0.0 191.2 jit_solution(15708558418689725650)
XLA Ops:
  0.7 183.3 %shard_map.306 = (bf16[512,768]{1,0:T(8,128)(2,1)}, bf16[512,768]{1,0:T(8,128)(2,1)}, bf16[256,768]{1,0:T(8,128)(2,1)}, f32[96,12672]{1,0:T(8,128)}) custom-call(s32[4]{0:T(128)} %refs_0_.1, s32[4,10]{1,0:T(4,128)} %refs_1_.1, f32[768]{0:T(1024)} %refs_2_.1, f32[768]{0:T(1024)} %refs_3_.1, f32[768]{0:T(1024)} %refs_4_.2, f32[12,32]{1,0:T(8,128)} %bitcast.14, ...), custom_call_target="tpu_custom_call" | custom-call | flops 30000001024 | bytes 35000000 | tf_op jit(solution)/shard_map/pallas_call | solution.py:929
  184.0 7.0 %shard_map.307 = (bf16[512,768]{1,0:T(8,128)(2,1)}, bf16[512,768]{1,0:T(8,128)(2,1)}, bf16[256,768]{1,0:T(8,128)(2,1)}, f32[96,3072]{1,0:T(8,128)}, f32[384,768]...) custom-call(bf16[512,768]{1,0:T(8,128)(2,1)} %get-tuple-element.36.r, ...), custom_call_target="tpu_custom_call" | custom-call | bytes 15000000 | tf_op jit(solution)/shard_map/pallas_call | solution.py:929

commit v3 on v2

--- a/solution.py
+++ b/solution.py
@@ -88,8 +88,7 @@
 
 
 class Layer:
-    def __init__(self, given, hbm, out, vm, load, store):
-        vars(self).update(vars(given))
+    def __init__(self, hbm, out, vm, load, store):
         vars(self).update(vars(vm))
         self.hbm, self.out, self.store = hbm, out, store
         self.layer_output, self.grad_tokens = vm.cotangent, vm.att2
@@ -158,9 +157,12 @@
 
     def forward(self, enter):
         load = self.load
-        for copy in (load.tokens, load.self_qkv, load.encodings, load.cross_kv):
+        few = (load.gain_self, load.gain_cross, load.gain_ff, load.rel_bias, load.tables, load.lengths, load.ids)
+        for copy in (load.tokens, load.self_qkv) + few + (load.encodings, load.cross_kv):
             copy.start()
         enter()
+        for copy in few:
+            copy.wait()
         for n, gain in enumerate((self.gain_self, self.gain_cross, self.gain_ff)):
             self.gains[n:n + 1, :] = gain[...].reshape(1, gain.shape[0])
         right = self.right
@@ -519,7 +521,9 @@
         bar = pltpu.get_barrier_semaphore()
         for target in (self.to_core, self.to_x, self.to_y, self.to_pair, self.to_mid):
             pl.semaphore_signal(bar, inc=1, device_id=target, device_id_type=MESH_ID)
-        pl.semaphore_wait(bar, 5)
+
+    def entered(self):
+        pl.semaphore_wait(pltpu.get_barrier_semaphore(), 5)
 
     def copy(self, src, dst, send, recv, target):
         return pltpu.make_async_remote_copy(
@@ -571,9 +575,8 @@
 
     def result(self, k, n):
         if n == SMALL_ROWS:
-            last = k == LAST
-            u = k - SMALL_FROM
-            row, d = jnp.where(last, 0, lax.rem(u, 2) * SMALL_ROWS), jnp.where(last, CHUNKS, CHUNKS - SPLIT + u // 2)
+            sums, u = k == SMALL_FROM, k - SMALL_FROM - 1
+            row, d = jnp.where(sums, 0, lax.rem(u + 2, 2) * SMALL_ROWS), jnp.where(sums, CHUNKS, CHUNKS - SPLIT + u // 2)
         else:
             row, d = 0, data_of(k)
         return self.out.at[pl.ds(pl.multiple_of(row, 8), n), pl.ds(pl.multiple_of(d * CHUNK_COLS, LANES), CHUNK_COLS)]
@@ -796,14 +799,14 @@
         self.fill(t, half_product)
 
     def finish(self, half, small):
+        self.move(SMALL_FROM)
+        self.fill_small(jnp.int32(SMALL_FROM), lambda parity: small[parity])
+
         def body(k, c):
             self.move(k)
-            self.fill_small(k, lambda parity: half(parity, k - SMALL_FROM))
-            return c
-        lax.fori_loop(SMALL_FROM, LAST, body, 0)
-        self.move(LAST)
-        self.fill_small(LAST, lambda parity: small[parity])
-
+            self.fill_small(k, lambda parity: half(parity, k - SMALL_FROM - 1))
+            return c
+        lax.fori_loop(SMALL_FROM + 1, LAST + 1, body, 0)
         self.drain()
         for back in range(DEPTH.snd):
             self.core_copy(LAST - back, SMALL_ROWS).wait_send()
@@ -834,6 +837,9 @@
     def enter(self):
         pass
 
+    def entered(self):
+        pass
+
     def step(self, t, half_product):
         for parity in range(2):
             value = half_product(parity)
@@ -853,11 +859,12 @@
 
 
 def layer_kernel(groups, alone, *refs):
-    given, hbm, out, vm, load, store, bufs, sems = regroup(groups, refs)
+    hbm, out, vm, load, store, bufs, sems = regroup(groups, refs)
     reducer = (PartWriter if alone else Reducer)(bufs, sems, out.chunks)
-    layer = Layer(given, hbm, out, vm, load, store)
+    layer = Layer(hbm, out, vm, load, store)
     layer.reducer = reducer
     layer.forward(reducer.enter)
+    reducer.entered()
     layer.feed_forward()
     layer.backward_cross()
     layer.backward_self()
@@ -936,7 +943,7 @@
     return Bunch(**{name: (value, space) for name, value in values.items()})
 
 
-def run_layer(alone, hbm, given, tables):
+def run_layer(alone, hbm):
     rows, width = hbm.tokens.shape
     enc_rows = hbm.encodings.shape[0]
     entries = hbm.memory_keys.shape[0]
@@ -951,7 +958,8 @@
     else:
         vars(outs).update(vars(in_space(pl.ANY, chunks=shape((CHUNK_ROWS, (CHUNKS + 1) * CHUNK_COLS), F32))))
     loaded = [name for name in vars(hbm) if vars(hbm)[name] is not hbm.ff_in and vars(hbm)[name] is not hbm.ff_out]
-    vm = Bunch(**{name: pltpu.VMEM(vars(hbm)[name].shape, BF16) for name in loaded})
+    place_of = lambda v: (pltpu.SMEM if v.dtype == jnp.int32 else pltpu.VMEM)(v.shape, v.dtype)
+    vm = Bunch(**{name: place_of(vars(hbm)[name]) for name in loaded})
     big = lambda cols, kind: pltpu.VMEM((rows, cols), kind)
     vars(vm).update(
         wi=pltpu.VMEM((2, width, FF_TILE), BF16), wo=pltpu.VMEM((2, FF_TILE, width), BF16),
@@ -975,10 +983,7 @@
         extra = {}
     else:
         vm.small = pltpu.VMEM((2, 4, SMALL_ROWS, CHUNK_COLS), F32)
-    ins = [Bunch(**vars(in_space(pltpu.SMEM, lengths=given.lengths, ids=given.ids)),
-                 **vars(in_space(pltpu.VMEM, gain_self=given.gain_self, gain_cross=given.gain_cross,
-                                 gain_ff=given.gain_ff, rel_bias=given.rel_bias, tables=tables))),
-           in_space(pl.ANY, **vars(hbm))]
+    ins = [in_space(pl.ANY, **vars(hbm))]
     return call_grouped(
         lambda groups, *refs: layer_kernel(groups, alone, *refs), ins, [outs], [vm, load, store, bufs, sems],
         compiler_params=pltpu.CompilerParams(has_side_effects=True, vmem_limit_bytes=62 * 2**20, **extra),
@@ -989,12 +994,14 @@
 
 
 def place_kernel(groups, *refs):
-    given, tables, out, vm = regroup(groups, refs)
+    given, out, vm = regroup(groups, refs)
     sems = iter(range(vm.sem.shape[0]))
     copy = lambda src, dst: pltpu.make_async_copy(src, dst, vm.sem.at[next(sems)])
     small_at = slice(CHUNKS * CHUNK_COLS, (CHUNKS + 1) * CHUNK_COLS)
     small = copy(given.chunks.at[0:SMALL_ROWS, small_at], vm.chunks.at[0:SMALL_ROWS, small_at])
+    table = copy(given.tables, vm.tables)
     small.start()
+    table.start()
     pieces = ((out.ff_in, FF_IN_AT), (out.ff_out, FF_OUT_AT), (out.cross_out, CROSS_OUT_AT), (out.cross_q, CROSS_Q_AT),
               (out.cross_kv, CROSS_KV_AT), (out.self_out, SELF_OUT_AT), (out.self_qkv, SELF_QKV_AT))
     moves = []
@@ -1013,21 +1020,24 @@
     for into, _ in moves:
         into.start()
     small.wait()
+    table.wait()
     sums = vm.chunks[0:SMALL_ROWS, small_at]
     for j in range(6):
         row, col = 8 * (j % 4), LANES * (j // 4)
-        out.mem_k[:, j * LANES:(j + 1) * LANES] = sums[row:row + 4, col:col + LANES]
-        out.mem_v[:, j * LANES:(j + 1) * LANES] = sums[row + 4:row + 8, col:col + LANES]
-    for n, gain in enumerate((out.gain_self, out.gain_cross, out.gain_ff)):
+        vm.mem_k[:, j * LANES:(j + 1) * LANES] = sums[row:row + 4, col:col + LANES]
+        vm.mem_v[:, j * LANES:(j + 1) * LANES] = sums[row + 4:row + 8, col:col + LANES]
+    for n, gain in enumerate((vm.gain_self, vm.gain_cross, vm.gain_ff)):
         gain[...] = sums[16 + n, LANES:LANES + 96]
-    out.rel_bias[...] = nt(sums[0:16, 2 * LANES:], tables.tables[1], precision=lax.Precision.HIGHEST)[0:12]
+    vm.rel_bias[...] = nt(sums[0:16, 2 * LANES:], vm.tables[1], precision=lax.Precision.HIGHEST)[0:12]
+    made = [copy(vars(vm)[name], vars(out)[name]) for name in vars(vm) if name in vars(out)]
+    for move in made:
+        move.start()
     for into, onward in moves:
         into.wait()
         for move in onward:
             move.start()
-    for _, onward in moves:
-        for move in onward:
-            move.wait()
+    for move in made + [move for _, onward in moves for move in onward]:
+        move.wait()
 
 
 def place(done, tables):
@@ -1037,16 +1047,15 @@
         grad_encodings=shape(done.grad_encodings.shape, BF16), ff_in=shape((96, 3072), F32), ff_out=shape((384, 768), F32),
         cross_out=shape((96, 768), F32), cross_q=shape((96, 768), F32), cross_kv=shape((96, 1536), F32),
         self_out=shape((96, 768), F32), self_qkv=shape((96, 2304), F32))
-    gain = shape((96,), F32)
-    vars(outs).update(vars(in_space(
-        pltpu.VMEM, mem_k=shape((4, 768), F32), mem_v=shape((4, 768), F32), gain_self=gain, gain_cross=gain,
-        gain_ff=gain, rel_bias=shape((12, 32), F32))))
+    small = Bunch(mem_k=(4, 768), mem_v=(4, 768), gain_self=(96,), gain_cross=(96,), gain_ff=(96,), rel_bias=(12, 32))
+    vars(outs).update(vars(in_space(pl.ANY, **{name: shape(dims, F32) for name, dims in vars(small).items()})))
     scratch = Bunch(
         chunks=pltpu.VMEM(done.chunks.shape, F32), a=pltpu.VMEM(done.layer_output.shape, BF16),
         b=pltpu.VMEM(done.grad_tokens.shape, BF16), c=pltpu.VMEM(done.grad_encodings.shape, BF16),
-        sem=pltpu.SemaphoreType.DMA((28,)))
+        tables=pltpu.VMEM(tables.shape, F32), sem=pltpu.SemaphoreType.DMA((36,)),
+        **{name: pltpu.VMEM(dims, F32) for name, dims in vars(small).items()})
     return call_grouped(
-        place_kernel, [in_space(pl.ANY, **vars(done)), in_space(pltpu.VMEM, tables=tables)], [outs], [scratch],
+        place_kernel, [in_space(pl.ANY, tables=tables, **vars(done))], [outs], [scratch],
         compiler_params=pltpu.CompilerParams(vmem_limit_bytes=62 * 2**20),
         cost_estimate=pl.CostEstimate(flops=0, bytes_accessed=15 * 10**6, transcendentals=0))
 
@@ -1076,14 +1085,13 @@
               rel_bias, self_qkv, self_out, cross_q, cross_kv, cross_out, ff_in, ff_out, cotangent):
     width = tokens.shape[-1]
     alone = not (lax.axis_size("dp") == 8 and lax.axis_size("replica") == 4)
+    tables = jnp.asarray(bucket_tables(LANES, rel_bias.shape[0]))
     hbm = Bunch(tokens=tokens.reshape(-1, width), encodings=encodings.reshape(-1, width),
                 cotangent=cotangent.reshape(-1, width), memory_keys=memory_keys, memory_values=memory_values,
                 self_qkv=self_qkv, self_out=self_out, cross_q=cross_q, cross_kv=cross_kv, cross_out=cross_out,
-                ff_in=ff_in, ff_out=ff_out)
-    given = Bunch(lengths=lengths, ids=memory_ids, gain_self=gain_self, gain_cross=gain_cross, gain_ff=gain_ff,
-                  rel_bias=rel_bias.T)
-    tables = jnp.asarray(bucket_tables(LANES, rel_bias.shape[0]))
-    done = run_layer(alone, hbm, given, tables)
+                ff_in=ff_in, ff_out=ff_out, lengths=lengths, ids=memory_ids, gain_self=gain_self,
+                gain_cross=gain_cross, gain_ff=gain_ff, rel_bias=rel_bias.T, tables=tables)
+    done = run_layer(alone, hbm)
     out = sum_alone(done, tables) if alone else place(done, tables)
     return (
         out.layer_output.reshape(tokens.shape), out.grad_tokens.reshape(tokens.shape),

time: 191 us -> 190 us (level)
  no operation moved by 1% of the time
where the time goes in v3:
time: 190 us
  Pallas kernels  189 us (99%)
    pallas_call x2, Pallas kernels, call_grouped(): pl.pallas_call(functools.partial(kernel, groups), out_shape=pairs(outs, 0...  189 us

profile of v3, /device:TPU:0, one launch (start us, length us, event | category | flops | bytes accessed | tf_op | source)
XLA Modules:
  0.0 189.6 jit_solution(15337449549901795055)
XLA Ops:
  0.7 183.0 %shard_map.306 = (bf16[512,768]{1,0:T(8,128)(2,1)}, bf16[512,768]{1,0:T(8,128)(2,1)}, bf16[256,768]{1,0:T(8,128)(2,1)}, f32[96,12672]{1,0:T(8,128)}) custom-call(bf16[512,768]{1,0:T(8,128)(2,1)} %bitcast.8, bf16[256,768]{1,0:T(8,128)(2,1)} %bitcast.12, bf16[512,768]{1,0:T(8,128)(2,1)} %bitcast.9, bf16[32,768]{1,0:T(8,128)(2,1)} %refs_3_.1, ...), custom_call_target="tpu_custom_call" | custom-call | flops 30000001024 | bytes 35000000 | tf_op jit(solution)/shard_map/pallas_call | solution.py:936
  183.7 5.8 %shard_map.307 = (bf16[512,768]{1,0:T(8,128)(2,1)}, bf16[512,768]{1,0:T(8,128)(2,1)}, bf16[256,768]{1,0:T(8,128)(2,1)}, f32[96,3072]{1,0:T(8,128)}, f32[384,768]...) custom-call(f32[2,32,128]{2,1,0:T(8,128)} %constant.2.clone.refs_18_, ...), custom_call_target="tpu_custom_call" | custom-call | bytes 15000000 | tf_op jit(solution)/shard_map/pallas_call | solution.py:936

commit v4 on v3

--- a/solution.py
+++ b/solution.py
@@ -482,7 +482,7 @@
 
 
 MESH_ID = pl.DeviceIdType.MESH
-CHUNK_ROWS, CHUNK_COLS, PAIR_ROWS, SMALL_ROWS = 96, 384, 48, 48
+CHUNK_ROWS, CHUNK_COLS, PAIR_ROWS, SMALL_ROWS, SUM_ROWS = 96, 384, 48, 48, 32
 PERIOD, GAP, LAST_PAIR, SMALL_FROM, LAST = 5, 26, 21, 29, 37
 CHUNKS, SPLIT = 32, 4
 DEPTH = Bunch(own=12, mid=10, snd=3, r0=3, rp=2, r1=6, r2=5, r3=5, r4=5)
@@ -497,6 +497,10 @@
 def data_of(k):
     pair = (lax.rem(k, PERIOD) == 1) & (k <= GAP)
     return jnp.where(pair, k - PERIOD, jnp.where(k > GAP, k - 1, k))
+
+
+def rows_of(k):
+    return CHUNK_ROWS if k < SMALL_FROM else SUM_ROWS if k == SMALL_FROM else SMALL_ROWS
 
 
 class Reducer:
@@ -574,9 +578,11 @@
         return self.copy(self.mine(k, n), self.b.r4.at[r, pl.ds(0, n)], self.s.s4.at[r], self.s.r4.at[r], self.to_mid)
 
     def result(self, k, n):
-        if n == SMALL_ROWS:
-            sums, u = k == SMALL_FROM, k - SMALL_FROM - 1
-            row, d = jnp.where(sums, 0, lax.rem(u + 2, 2) * SMALL_ROWS), jnp.where(sums, CHUNKS, CHUNKS - SPLIT + u // 2)
+        if n == SUM_ROWS:
+            row, d = 0, CHUNKS
+        elif n == SMALL_ROWS:
+            u = k - SMALL_FROM - 1
+            row, d = lax.rem(u, 2) * SMALL_ROWS, CHUNKS - SPLIT + u // 2
         else:
             row, d = 0, data_of(k)
         return self.out.at[pl.ds(pl.multiple_of(row, 8), n), pl.ds(pl.multiple_of(d * CHUNK_COLS, LANES), CHUNK_COLS)]
@@ -622,17 +628,20 @@
         for g in range(4):
             self.b.own[o, g // 2, g % 2] = here[g * n:(g + 1) * n]
 
-    def fill_small(self, k, part):
-        n = SMALL_ROWS
+    def fill_small(self, k, n, part):
         a, o = lax.rem(k, DEPTH.snd), lax.rem(k, DEPTH.own)
 
         @pl.when(k - DEPTH.snd < SMALL_FROM)
         def _():
             self.core_copy(self.before(k), CHUNK_ROWS).wait_send()
 
-        @pl.when(k - DEPTH.snd >= SMALL_FROM)
-        def _():
-            self.core_copy(k - DEPTH.snd, n).wait_send()
+        @pl.when(k - DEPTH.snd == SMALL_FROM)
+        def _():
+            self.core_copy(k - DEPTH.snd, SUM_ROWS).wait_send()
+
+        @pl.when(k - DEPTH.snd > SMALL_FROM)
+        def _():
+            self.core_copy(k - DEPTH.snd, SMALL_ROWS).wait_send()
         self.b.snd[a, :, 0:n, :] = part(1 - self.core)
 
         @pl.when(k != GAP + DEPTH.r0)
@@ -688,20 +697,21 @@
         o, r, half = lax.rem(k, DEPTH.own), lax.rem(k, DEPTH.r1), n // 2
         low, high = pl.ds(base, half), pl.ds(base + half, half)
         by_x, by_y = self.first_copies(k, n, base)
+        on_x, on_y = self.second_copies(k, n, base)
+        self.need(self.s.c2x, k, DEPTH.r2)
+        self.need(self.s.c2y, k, DEPTH.r2)
         by_x.wait_recv()
         for g in range(2):
             self.b.own[o, g, self.x, low, :] += self.b.r1x[r, g, 0:half]
+        on_y.start()
         by_y.wait_recv()
         for g in range(2):
             self.b.own[o, self.y, g, high, :] += self.b.r1y[r, g, 0:half]
+        on_x.start()
         self.grant(self.s.c1x, k, DEPTH.r1, self.to_x)
         self.grant(self.s.c1y, k, DEPTH.r1, self.to_y)
         by_x.wait_send()
         by_y.wait_send()
-        self.need(self.s.c2x, k, DEPTH.r2)
-        self.need(self.s.c2y, k, DEPTH.r2)
-        for copy in self.second_copies(k, n, base):
-            copy.start()
 
     def stage_three(self, k, n, base):
         o, r, half = lax.rem(k, DEPTH.own), lax.rem(k, DEPTH.r2), n // 2
@@ -712,15 +722,15 @@
         self.b.mid[m, high, :] = self.b.own[o, self.y, self.x, high, :] + self.b.r2x[r, 0:half]
         by_y.wait_recv()
         self.b.mid[m, low, :] = self.b.own[o, self.y, self.x, low, :] + self.b.r2y[r, 0:half]
+
+        @pl.when(self.end)
+        def _():
+            self.need(self.s.c3, k, DEPTH.r3)
+            self.inward_copy(k, n, base).start()
         self.grant(self.s.c2x, k, DEPTH.r2, self.to_x)
         self.grant(self.s.c2y, k, DEPTH.r2, self.to_y)
         by_x.wait_send()
         by_y.wait_send()
-
-        @pl.when(self.end)
-        def _():
-            self.need(self.s.c3, k, DEPTH.r3)
-            self.inward_copy(k, n, base).start()
 
     def stage_four(self, k, n, paired):
         r = lax.rem(k, DEPTH.r3)
@@ -737,9 +747,9 @@
                 self.b.mid[lax.rem(k, DEPTH.mid), pl.ds(self.far, part), :] = self.b.r3[r, 0:part]
             else:
                 self.mine(k, n)[...] += self.b.r3[r, 0:n]
-            self.grant(self.s.c3, k, DEPTH.r3, self.to_pair)
             self.need(self.s.c4, k, DEPTH.r4)
             self.middle_copy(k, n).start()
+            self.grant(self.s.c3, k, DEPTH.r3, self.to_pair)
 
     def stage_five(self, k, n):
         r = lax.rem(k, DEPTH.r4)
@@ -748,9 +758,9 @@
         def _():
             self.middle_copy(k, n).wait()
             self.mine(k, n)[...] += self.b.r4[r, 0:n]
-            self.grant(self.s.c4, k, DEPTH.r4, self.to_mid)
             self.outward_copy(k, n).start()
             self.keep_copy(k, n).start()
+            self.grant(self.s.c4, k, DEPTH.r4, self.to_mid)
 
     def stage_six(self, k, n):
         @pl.when(self.inner)
@@ -759,29 +769,27 @@
         self.keep_copy(k, n).wait()
 
     def stages(self):
-        n, small, pair = CHUNK_ROWS, SMALL_ROWS, PAIR_ROWS
+        pair = PAIR_ROWS
         return (
-            (lambda k: self.stage_one(k, n), self.stage_one_pair, lambda k: self.stage_one(k, small)),
-            (lambda k: self.stage_two(k, n, 0), lambda k: self.stage_two(k, pair, self.near),
-             lambda k: self.stage_two(k, small, 0)),
-            (lambda k: self.stage_three(k, n, 0), lambda k: self.stage_three(k, pair, self.near),
-             lambda k: self.stage_three(k, small, 0)),
-            (lambda k: self.stage_four(k, n, False), lambda k: self.stage_four(k, n, True),
-             lambda k: self.stage_four(k, small, False)),
-            (lambda k: self.stage_five(k, n), None, lambda k: self.stage_five(k, small)),
-            (lambda k: self.stage_six(k, n), None, lambda k: self.stage_six(k, small)),
+            (lambda n, k: self.stage_one(k, n), self.stage_one_pair),
+            (lambda n, k: self.stage_two(k, n, 0), lambda k: self.stage_two(k, pair, self.near)),
+            (lambda n, k: self.stage_three(k, n, 0), lambda k: self.stage_three(k, pair, self.near)),
+            (lambda n, k: self.stage_four(k, n, False), lambda k: self.stage_four(k, CHUNK_ROWS, True)),
+            (lambda n, k: self.stage_five(k, n), None),
+            (lambda n, k: self.stage_six(k, n), None),
         )
 
     def move(self, t):
-        for behind, (usual, paired, small) in reversed(list(zip(after(LAG), self.stages()))):
+        for behind, (usual, paired) in reversed(list(zip(after(LAG), self.stages()))):
             k = t - behind
             odd = (lax.rem(k + PERIOD, PERIOD) == 1) & (k <= GAP)
-            if paired is None:
-                pl.when((k >= 0) & (k < SMALL_FROM) & (k != 1))(functools.partial(usual, k))
-            else:
-                pl.when((k >= 0) & (k < SMALL_FROM) & jnp.logical_not(odd))(functools.partial(usual, k))
+            plain = (k >= 0) & (k < SMALL_FROM) & (k != 1)
+            if paired is not None:
+                plain = plain & jnp.logical_not(odd)
                 pl.when(odd & (k > 1))(functools.partial(paired, k))
-            pl.when((k >= SMALL_FROM) & (k <= LAST))(functools.partial(small, k))
+            pl.when(plain)(functools.partial(usual, CHUNK_ROWS, k))
+            pl.when(k == SMALL_FROM)(functools.partial(usual, SUM_ROWS, k))
+            pl.when((k > SMALL_FROM) & (k <= LAST))(functools.partial(usual, SMALL_ROWS, k))
         d = t - LAG.one
         pl.when((lax.rem(d + PERIOD, PERIOD) == 1) & (d >= 0) & (d <= LAST_PAIR))(functools.partial(self.stage_pair, d))
 
@@ -790,9 +798,11 @@
         for number, (due, order) in enumerate(zip(after(LAG), after(LATE))):
             left += [(k + order, -number, k) for k in range(LAST + 1) if k + due > LAST]
         for _, number, k in sorted(left):
-            usual, paired, small = self.stages()[-number]
-            odd = k % PERIOD == 1 and k <= GAP
-            (small if k >= SMALL_FROM else paired if odd and paired is not None else usual)(jnp.int32(k))
+            usual, paired = self.stages()[-number]
+            if k % PERIOD == 1 and k <= GAP and paired is not None:
+                paired(jnp.int32(k))
+            else:
+                usual(rows_of(k), jnp.int32(k))
 
     def step(self, t, half_product):
         self.move(t)
@@ -800,11 +810,11 @@
 
     def finish(self, half, small):
         self.move(SMALL_FROM)
-        self.fill_small(jnp.int32(SMALL_FROM), lambda parity: small[parity])
+        self.fill_small(jnp.int32(SMALL_FROM), SUM_ROWS, lambda parity: small[parity])
 
         def body(k, c):
             self.move(k)
-            self.fill_small(k, lambda parity: half(parity, k - SMALL_FROM - 1))
+            self.fill_small(k, SMALL_ROWS, lambda parity: half(parity, k - SMALL_FROM - 1))
             return c
         lax.fori_loop(SMALL_FROM + 1, LAST + 1, body, 0)
         self.drain()
@@ -926,7 +936,6 @@
         block[24:32, LANES:2 * LANES] = jnp.zeros((8, LANES), F32)
         block[0:16, 2 * LANES:] = bias
         block[16:32, 2 * LANES:] = jnp.zeros((16, LANES), F32)
-        block[32:, :] = jnp.zeros((SMALL_ROWS - 32, CHUNK_COLS), F32)
 
 
 def call_grouped(kernel, ins, outs, scratch, **options):
@@ -982,7 +991,7 @@
         bufs, sems = Bunch(own=pltpu.VMEM((2, 2, 2, CHUNK_ROWS, CHUNK_COLS), F32)), Bunch(out=pltpu.SemaphoreType.DMA((1,)))
         extra = {}
     else:
-        vm.small = pltpu.VMEM((2, 4, SMALL_ROWS, CHUNK_COLS), F32)
+        vm.small = pltpu.VMEM((2, 4, SUM_ROWS, CHUNK_COLS), F32)
     ins = [in_space(pl.ANY, **vars(hbm))]
     return call_grouped(
         lambda groups, *refs: layer_kernel(groups, alone, *refs), ins, [outs], [vm, load, store, bufs, sems],
@@ -998,7 +1007,7 @@
     sems = iter(range(vm.sem.shape[0]))
     copy = lambda src, dst: pltpu.make_async_copy(src, dst, vm.sem.at[next(sems)])
     small_at = slice(CHUNKS * CHUNK_COLS, (CHUNKS + 1) * CHUNK_COLS)
-    small = copy(given.chunks.at[0:SMALL_ROWS, small_at], vm.chunks.at[0:SMALL_ROWS, small_at])
+    small = copy(given.chunks.at[0:SUM_ROWS, small_at], vm.chunks.at[0:SUM_ROWS, small_at])
     table = copy(given.tables, vm.tables)
     small.start()
     table.start()
@@ -1021,7 +1030,7 @@
         into.start()
     small.wait()
     table.wait()
-    sums = vm.chunks[0:SMALL_ROWS, small_at]
+    sums = vm.chunks[0:SUM_ROWS, small_at]
     for j in range(6):
         row, col = 8 * (j % 4), LANES * (j // 4)
         vm.mem_k[:, j * LANES:(j + 1) * LANES] = sums[row:row + 4, col:col + LANES]

time: 190 us -> 189 us (level)
  no operation moved by 1% of the time
where the time goes in v4:
time: 189 us
  Pallas kernels  188 us (99%)
    pallas_call x2, Pallas kernels, call_grouped(): pl.pallas_call(functools.partial(kernel, groups), out_shape=pairs(outs, 0...  188 us

profile of v4, /device:TPU:0, one launch (start us, length us, event | category | flops | bytes accessed | tf_op | source)
XLA Modules:
  0.0 189.3 jit_solution(17798283958129870791)
XLA Ops:
  0.7 182.6 %shard_map.306 = (bf16[512,768]{1,0:T(8,128)(2,1)}, bf16[512,768]{1,0:T(8,128)(2,1)}, bf16[256,768]{1,0:T(8,128)(2,1)}, f32[96,12672]{1,0:T(8,128)}) custom-call(bf16[512,768]{1,0:T(8,128)(2,1)} %bitcast.8, bf16[256,768]{1,0:T(8,128)(2,1)} %bitcast.12, bf16[512,768]{1,0:T(8,128)(2,1)} %bitcast.9, bf16[32,768]{1,0:T(8,128)(2,1)} %refs_3_.1, ...), custom_call_target="tpu_custom_call" | custom-call | flops 30000001024 | bytes 35000000 | tf_op jit(solution)/shard_map/pallas_call | solution.py:945
  183.3 5.8 %shard_map.307 = (bf16[512,768]{1,0:T(8,128)(2,1)}, bf16[512,768]{1,0:T(8,128)(2,1)}, bf16[256,768]{1,0:T(8,128)(2,1)}, f32[96,3072]{1,0:T(8,128)}, f32[384,768]...) custom-call(f32[2,32,128]{2,1,0:T(8,128)} %constant.2.clone.refs_18_, ...), custom_call_target="tpu_custom_call" | custom-call | bytes 15000000 | tf_op jit(solution)/shard_map/pallas_call | solution.py:945
